TPU v7x, 128 devices: a whole 4x4x4 slice. The times are simulated.
128 devices in a mesh: lat: 8 (over z, y_lo), lon: 16 (over y_hi, x, core).
Axes of the slice: x: 4, y: 4 (y_hi: 2, y_lo: 2; y = y_hi * 2 + y_lo), z: 4, core: 2. Of those that a mesh axis runs over, the one named last changes fastest.
Arguments:
- tokens: bfloat16 [4, 48, 384, 512], P(None, 'lat', 'lon'), may hold values from -6 to 6
- cotangent: bfloat16 [4, 48, 384, 512], P(None, 'lat', 'lon'), may hold values from -6 to 6
- w_qkv: bfloat16 [512, 1536], replicated, may hold values from -12 to 12
- w_proj: bfloat16 [512, 512], replicated, may hold values from -0.25 to 0.25
Outputs:
- output: bfloat16 [4, 48, 384, 512], P(None, 'lat', 'lon')
- grad_tokens: bfloat16 [4, 48, 384, 512], P(None, 'lat', 'lon')
- grad_qkv: float32 [512, 1536], replicated
- grad_proj: float32 [512, 512], replicated
All inputs are finite; a program needn't handle non-finite values.
Results may differ from a plain program's by a relative error of at most 0.011.
Values may be sent and summed in bfloat16 or wider, within the bound.
A program may use at most 128 MiB of HBM per device.

v0:
```python
import functools
import numpy as np
import jax
import jax.numpy as jnp
from jax import lax
from jax.experimental import pallas as pl
from jax.experimental.pallas import tpu as pltpu

HEADS = 16
BF = jnp.bfloat16
F32 = jnp.float32
SCALE = 1.0 / 32**0.5
EXP2 = SCALE * 1.4426950408889634
NT = (((1,), (1,)), ((), ()))
TN = (((0,), (0,)), ((), ()))


def dot(a, b, dims=(((1,), (0,)), ((), ()))):
    return lax.dot_general(a, b, dims, preferred_element_type=F32)


def head_mask(dtype):
    head = lax.broadcasted_iota(jnp.int32, (128, 256), 0) >> 4
    col = lax.broadcasted_iota(jnp.int32, (128, 256), 1) >> 5
    return (head == col).astype(dtype)


def project(w, tok, cot, w_qkv, w_proj, hat, normed, inv, q, k, v, dc):
    x = tok[w].astype(F32)
    x = x - jnp.mean(x, axis=1, keepdims=True)
    scale = lax.rsqrt(jnp.mean(x * x, axis=1, keepdims=True) + 1e-05)
    x = x * scale
    hat[w] = x
    inv[w] = jnp.broadcast_to(scale, (144, 128))
    x = x.astype(BF)
    rows = pl.ds(pl.multiple_of(w * 144, 16), 144)
    normed[rows, :] = x
    for part, ref in enumerate((q, k, v)):
        for g in range(2):
            at = 512 * part + 256 * g
            ref[g, w] = dot(x, w_qkv[:, at : at + 256]).astype(BF)
    c = cot[rows, :]
    for g in range(2):
        dc[g, w] = dot(c, w_proj[256 * g : 256 * g + 256, :], NT).astype(BF)


def attend(g, w, klab, qlab, mask, maskf, q, k, v, dc, qs, cs, pt, st, ctx, dqkv, sf, df):
    keys = k[g, w]
    vals = v[g, w]
    rows0 = pl.multiple_of(w * 144, 16)
    for c in range(9):
        at = slice(128 * c, 128 * c + 128)
        q16 = q[g, w, 16 * c : 16 * c + 16, :]
        d16 = dc[g, w, 16 * c : 16 * c + 16, :]
        qs[at, :] = jnp.concatenate([q16] * 8, axis=0) * mask
        cs[at, :] = jnp.concatenate([d16] * 8, axis=0) * mask
    sf[...] = dot(keys, qs[...], NT)
    df[...] = dot(vals, cs[...], NT)
    for c in range(9):
        at = slice(128 * c, 128 * c + 128)
        s = sf[:, at]
        s = jnp.where(klab == qlab[c], s, -1e30)
        e = jnp.exp2((s - jnp.max(s, axis=0, keepdims=True)) * EXP2)
        p = e * (1.0 / jnp.sum(e, axis=0, keepdims=True))
        pt[:, at] = p.astype(BF)
        dp = df[:, at]
        inner = jnp.sum(p * dp, axis=0, keepdims=True)
        st[:, at] = ((p * SCALE) * (dp - inner)).astype(BF)
    out = dot(pt[...], vals, TN).reshape(9, 8, 16, 256) * maskf.reshape(1, 8, 16, 256)
    ctx[g, pl.ds(rows0, 144), :] = jnp.sum(out, axis=1).reshape(144, 256).astype(BF)
    out = dot(st[...], keys, TN).reshape(9, 8, 16, 256) * maskf.reshape(1, 8, 16, 256)
    dqkv[g, pl.ds(rows0, 144), 0:256] = jnp.sum(out, axis=1).reshape(144, 256).astype(BF)
    rows = pl.ds(rows0, 144)
    dqkv[g, rows, 256:512] = dot(st[...], qs[...]).astype(BF)
    dqkv[g, rows, 512:768] = dot(pt[...], cs[...]).astype(BF)


def finish(w, w_qkv, w_proj, hat, inv, ctx, dqkv, att, dflat):
    rows = pl.ds(pl.multiple_of(w * 144, 16), 144)
    a = dot(ctx[0, rows, :], w_proj[0:256, :]) + dot(ctx[1, rows, :], w_proj[256:512, :])
    att[w] = a.astype(BF)
    d = None
    for g in range(2):
        for part in range(3):
            at = 512 * part + 256 * g
            t = dot(dqkv[g, rows, 256 * part : 256 * part + 256], w_qkv[:, at : at + 256], NT)
            d = t if d is None else d + t
    h = hat[w]
    d = d - jnp.mean(d, axis=1, keepdims=True) - h * jnp.mean(d * h, axis=1, keepdims=True)
    scale = jnp.concatenate([inv[w]] * 4, axis=1)
    dflat[w] = (d * scale).astype(BF)


def labels(w, lat_last, lon_last):
    def flags(t):
        level = (t >= 72).astype(jnp.int32)
        t = t - 72 * level
        row = (t >= 36).astype(jnp.int32)
        t = t - 36 * row
        t = jnp.where(t >= 24, t - 24, jnp.where(t >= 12, t - 12, t))
        col = (t >= 6).astype(jnp.int32)
        return level * is_b + row * lat_last + col * last

    is_b = 4 * (w // 2)
    last = lon_last * (w % 2)
    klab = flags(lax.broadcasted_iota(jnp.int32, (144, 128), 0))
    lane = lax.broadcasted_iota(jnp.int32, (1, 128), 1) & 15
    qlab = [flags(lane + 16 * c) for c in range(9)]
    return klab, qlab


def kernel(tok, cot, w_qkv, w_proj, att, dflat, gqkv, gproj, hat, normed, inv, q, k, v, dc, qs, cs, pt, st, ctx, dqkv, sf, df):
    lat_last = 2 * (lax.axis_index("lat") == lax.axis_size("lat") - 1).astype(jnp.int32)
    lon_last = (lax.axis_index("lon") == lax.axis_size("lon") - 1).astype(jnp.int32)

    @pl.loop(0, 4)
    def _(w):
        project(w, tok, cot, w_qkv, w_proj, hat, normed, inv, q, k, v, dc)

    mask = head_mask(BF)
    maskf = head_mask(F32)

    @pl.loop(0, 8)
    def _(i):
        g, w = i // 4, i % 4
        klab, qlab = labels(w, lat_last, lon_last)
        attend(g, w, klab, qlab, mask, maskf, q, k, v, dc, qs, cs, pt, st, ctx, dqkv, sf, df)

    for g in range(2):
        gproj[256 * g : 256 * g + 256, :] = dot(ctx[g], cot[...], TN)
        for part in range(3):
            gqkv[:, 512 * part + 256 * g : 512 * part + 256 * g + 256] = dot(
                normed[...], dqkv[g, :, 256 * part : 256 * part + 256], TN
            )

    @pl.loop(0, 4)
    def _(w):
        finish(w, w_qkv, w_proj, hat, inv, ctx, dqkv, att, dflat)


def local_block(tok, cot, w_qkv, w_proj):
    vm = pl.BlockSpec(memory_space=pltpu.VMEM)
    return pl.pallas_call(
        kernel,
        out_shape=(
            jax.ShapeDtypeStruct((4, 144, 512), BF),
            jax.ShapeDtypeStruct((4, 144, 512), BF),
            jax.ShapeDtypeStruct((512, 1536), F32),
            jax.ShapeDtypeStruct((512, 512), F32),
        ),
        in_specs=[vm] * 4,
        out_specs=(vm,) * 4,
        scratch_shapes=[
            pltpu.VMEM((4, 144, 512), F32),
            pltpu.VMEM((576, 512), BF),
            pltpu.VMEM((4, 144, 128), F32),
            pltpu.VMEM((2, 4, 144, 256), BF),
            pltpu.VMEM((2, 4, 144, 256), BF),
            pltpu.VMEM((2, 4, 144, 256), BF),
            pltpu.VMEM((2, 4, 144, 256), BF),
            pltpu.VMEM((1152, 256), BF),
            pltpu.VMEM((1152, 256), BF),
            pltpu.VMEM((144, 1152), BF),
            pltpu.VMEM((144, 1152), BF),
            pltpu.VMEM((2, 576, 256), BF),
            pltpu.VMEM((2, 576, 768), BF),
            pltpu.VMEM((144, 1152), F32),
            pltpu.VMEM((144, 1152), F32),
        ],
        compiler_params=pltpu.CompilerParams(vmem_limit_bytes=56 * 2**20),
        name="window_block",
    )(tok, cot.reshape(576, 512), w_qkv, w_proj)
from jax.sharding import PartitionSpec as P


def shifted(value, axis, steps):
    count = lax.axis_size(axis)
    pairs = [(source, (source + steps) % count) for source in range(count)]
    return lax.ppermute(value, axis, pairs)


def to_windows(field):
    levels, rows, cols, width = field.shape
    field = field.reshape(levels // 2, 2, rows // 6, 6, cols // 12, 12, width)
    return field.transpose(0, 2, 4, 1, 3, 5, 6).reshape(-1, 144, width)


def from_windows(field, levels, rows, cols):
    field = field.reshape(levels // 2, rows // 6, cols // 12, 2, 6, 12, -1)
    return field.transpose(0, 3, 1, 4, 2, 5, 6).reshape(levels, rows, cols, -1)


def roll_in(x):
    x = jnp.concatenate([x[:, 3:], shifted(x[:, :3], "lat", -1)], axis=1)
    x = jnp.concatenate([x[:, :, 6:], shifted(x[:, :, :6], "lon", -1)], axis=2)
    return jnp.roll(x, -1, axis=0)


def roll_out(x):
    x = jnp.roll(x, 1, axis=0)
    x = jnp.concatenate([shifted(x[:, :, -6:], "lon", 1), x[:, :, :-6]], axis=2)
    return jnp.concatenate([shifted(x[:, -3:], "lat", 1), x[:, :-3]], axis=1)


def body(tokens, cotangent, w_qkv, w_proj):
    tok = to_windows(roll_in(tokens))
    cot = to_windows(roll_in(cotangent))
    att, dflat, gqkv, gproj = local_block(tok, cot, w_qkv, w_proj)
    att = roll_out(from_windows(att, 4, 6, 24))
    dflat = roll_out(from_windows(dflat, 4, 6, 24))
    output = (tokens.astype(F32) + att.astype(F32)).astype(BF)
    grad_tokens = (cotangent.astype(F32) + dflat.astype(F32)).astype(BF)
    gqkv, gproj = lax.psum((gqkv, gproj), ("lat", "lon"))
    norm = 1.0 / 73728**0.5
    return (output, grad_tokens, gqkv * norm, gproj * norm)


def solution(mesh):
    spec = P(None, "lat", "lon", None)
    return jax.shard_map(
        body,
        mesh=mesh,
        in_specs=(spec, spec, P(), P()),
        out_specs=(spec, spec, P(), P()),
        check_vma=False,
    )
```

profile of v0, /device:TPU:1, one launch (start us, length us, event | category | flops | bytes accessed | tf_op | source)
XLA Modules:
  0.0 233.2 jit_solution(9721278213509266777)
XLA Ops:
  7.2 0.0 copy-start.1
  7.2 0.0 all-reduce.3.cloned.1.call-start
  7.2 1.1 fusion.9
  8.4 5.7 %collective-permute-start = (bf16[4,3,24,512]{3,2,1,0:T(8,128)(2,1)S(1)}, bf16[4,3,24,512]{3,2,1,0:T(8,128)(2,1)S(1)}, u32[]{:S(2)}, u32[]{:S(2)}) collective-permute-start(bf16[4,3,24,512]{3,2,1,0:T(8,128)(2,1)S(1)} %get-tuple-element.25), channel_id=1, source_target_pairs={{0,112},{16,0},{32,16},{48,32},{64,48},{80,64},{96,80},{112,96},{1... | collective-permute-start | bytes 884744 | tf_op jit(solution)/shard_map/ppermute | solution.py:179
  14.0 0.0 copy-done.1
  14.1 0.2 collective-permute-start.2
  14.3 5.4 %collective-permute-done = bf16[4,3,24,512]{3,2,1,0:T(8,128)(2,1)S(1)} collective-permute-done((bf16[4,3,24,512]{3,2,1,0:T(8,128)(2,1)S(1)}, bf16[4,3,24,512]{3,2,1,0:T(8,128)(2,1)S(1)}, u32[]{:S(2)}, u32[]{:S(2)}) %collective-permute-start) | collective-permute-done | bytes 294944 | tf_op jit(solution)/shard_map/ppermute | solution.py:179
  19.7 2.8 %collective-permute-start.1 = (bf16[4,6,6,512]{3,2,1,0:T(8,128)(2,1)S(1)}, bf16[4,6,6,512]{3,2,1,0:T(8,128)(2,1)S(1)}, u32[]{:S(2)}, u32[]{:S(2)}) collective-permute-start(bf16[4,6,6,512]{3,2,1,0:T(8,128)(2,1)S(1)} %pad_maximum_fusion.5), channel_id=1, source_target_pairs={{0,15},{1,0},{2,1},{3,2},{4,3},{5,4},{6,5},{7,6},{8,7},{9,8},{10,9... | collective-permute-start | bytes 442376 | tf_op jit(solution)/shard_map/ppermute | solution.py:179
  22.5 3.5 %collective-permute-done.2 = bf16[4,3,24,512]{3,2,1,0:T(8,128)(2,1)S(1)} collective-permute-done((bf16[4,3,24,512]{3,2,1,0:T(8,128)(2,1)S(1)}, bf16[4,3,24,512]{3,2,1,0:T(8,128)(2,1)S(1)}, u32[]{:S(2)}, u32[]{:S(2)}) %collective-permute-start.2) | collective-permute-done | bytes 294944 | tf_op jit(solution)/shard_map/ppermute | solution.py:179
  26.0 0.7 pad_maximum_fusion.4
  26.7 1.5 collective-permute-start.3
  28.3 0.2 slice_maximum_fusion.1
  28.4 0.2 slice_maximum_fusion
  28.6 0.0 collective-permute-done.1
  28.6 0.1 fusion.5
  28.7 0.1 fusion.3
  28.8 0.5 copy.13
  29.2 0.2 reshape.29
  29.5 0.1 copy.25
  29.6 0.9 reshape.36.tok
  30.6 2.4 %collective-permute-done.3 = bf16[4,6,6,512]{3,2,1,0:T(8,128)(2,1)S(1)} collective-permute-done((bf16[4,6,6,512]{3,2,1,0:T(8,128)(2,1)}, bf16[4,6,6,512]{3,2,1,0:T(8,128)(2,1)S(1)}, u32[]{:S(2)}, u32[]{:S(2)}) %collective-permute-start.3) | collective-permute-done | bytes 147488 | tf_op jit(solution)/shard_map/ppermute | solution.py:179
  32.9 0.1 fusion.4
  33.0 0.1 fusion.2
  33.1 0.5 copy.15
  33.5 0.2 reshape.31
  33.8 0.1 copy.16
  33.9 0.9 reshape_reshape.3.cot
  34.9 22.1 %window_block.1 = (bf16[4,144,512]{2,1,0:T(8,128)(2,1)}, bf16[4,144,512]{2,1,0:T(8,128)(2,1)}, f32[512,1536]{1,0:T(8,128)}, f32[512,512]{1,0:T(8,128)}) custom-call(bf16[4,144,512]{2,1,0:T(8,128)(2,1)} %reshape.36.tok, bf16[576,512]{1,0:T(8,128)(2,1)} %reshape_reshape.3.cot, bf16[512,1536]{1,0:T(8,128)(2,1)} %w_qkv.1, bf16[512,512]{1,0:T(8,128)(2,1)} %w_proj.1), custom_call_target="tpu_custom_call" | custom-call | tf_op jit(solution)/shard_map/window_block/pallas_call | solution.py:143
  57.0 0.0 all-reduce.3.cloned.1.call-update
  57.0 1.0 copy-done.4
  58.1 0.5 copy.18
  58.5 0.2 reshape.32
  58.8 0.6 copy.19
  59.4 0.0 copy-start.3
  59.4 0.2 reshape.33
  59.6 0.3 slice.108
  59.9 0.2 pad_maximum_fusion.7
  60.1 0.3 collective-permute-start.4
  60.4 0.1 copy-done.3
  60.4 0.5 copy.21
  60.9 0.2 reshape.34
  61.1 0.6 copy.22
  61.8 0.2 reshape.35
  62.0 0.3 slice.112
  62.3 0.2 pad_maximum_fusion.6
  62.5 1.6 collective-permute-start.6
  64.1 1.8 collective-permute-done.4
  65.9 0.5 fusion.1
  66.4 0.2 fusion.7
  66.6 0.0 copy-start
  66.6 0.1 collective-permute-start.5
  66.7 1.3 collective-permute-done.6
  68.0 0.5 fusion
  68.6 0.2 fusion.6
  68.8 0.1 collective-permute-start.7
  68.9 9.8 %collective-permute-done.5 = bf16[4,3,24,512]{3,0,2,1:T(4,128)(2,1)S(1)} collective-permute-done((bf16[4,3,24,512]{3,0,2,1:T(4,128)(2,1)S(1)}, bf16[4,3,24,512]{3,0,2,1:T(4,128)(2,1)S(1)}, u32[]{:S(2)}, u32[]{:S(2)}) %collective-permute-start.5) | collective-permute-done | bytes 294944 | tf_op jit(solution)/shard_map/ppermute | solution.py:179
  78.6 0.6 add_convert_fusion.1
  79.2 0.9 copy.23
  80.2 6.3 %collective-permute-done.7 = bf16[4,3,24,512]{3,0,2,1:T(4,128)(2,1)S(1)} collective-permute-done((bf16[4,3,24,512]{3,0,2,1:T(4,128)(2,1)S(1)}, bf16[4,3,24,512]{3,0,2,1:T(4,128)(2,1)S(1)}, u32[]{:S(2)}, u32[]{:S(2)}) %collective-permute-start.7) | collective-permute-done | bytes 294944 | tf_op jit(solution)/shard_map/ppermute | solution.py:179
  86.5 0.6 add_convert_fusion
  87.1 0.9 copy.24
  88.0 133.3 %all-reduce.3.cloned.1.call-done = (f32[512,1536]{1,0:T(8,128)}, f32[512,512]{1,0:T(8,128)}) async-done(((f32[512,1536]{1,0:T(8,128)}, f32[512,512]{1,0:T(8,128)}), (f32[512,1536]{1,0:T(8,128)}, f32[512,512]{1,0:T(8,128)})) %all-reduce.3.cloned.1.call-update) | async-done | bytes 4194320 | tf_op jit(solution)/shard_map/psum | solution.py:213
  221.3 4.0 %broadcast_multiply_fusion = f32[512,1536]{1,0:T(8,128)} fusion(f32[512,1536]{1,0:T(8,128)} %get-tuple-element.16), kind=kLoop, calls=%fused_computation | loop fusion | flops 786432 | bytes 6291456 | tf_op jit(solution)/shard_map/mul | solution.py:215
  225.2 1.1 broadcast_multiply_fusion.1
  (6 shorter events, 0.1 us)
Async XLA Ops:
  7.2 6.9 %copy-start.1 = (bf16[4,6,24,512]{3,2,1,0:T(8,128)(2,1)S(1)}, bf16[4,6,24,512]{3,2,1,0:T(8,128)(2,1)}, u32[]{:S(2)}) copy-start(bf16[4,6,24,512]{3,2,1,0:T(8,128)(2,1)} %param.5) | copy-start | bytes 1769476
  7.2 214.1 %all-reduce.3.cloned.1.call-start = ((), (), s32[]{:S(2)}) async-start(), calls=%async_computation | async-start | bytes 8388608 | tf_op jit(solution)/shard_map/psum | solution.py:213
  8.4 11.3 %collective-permute-start = (bf16[4,3,24,512]{3,2,1,0:T(8,128)(2,1)S(1)}, bf16[4,3,24,512]{3,2,1,0:T(8,128)(2,1)S(1)}, u32[]{:S(2)}, u32[]{:S(2)}) collective-permute-start(bf16[4,3,24,512]{3,2,1,0:T(8,128)(2,1)S(1)} %get-tuple-element.25), channel_id=1, source_target_pairs={{0,112},{16,0},{32,16},{48,32},{64,48},{80,64},{96,80},{112,96},{1... | collective-permute-start | bytes 884744 | tf_op jit(solution)/shard_map/ppermute | solution.py:179
  14.1 12.0 %collective-permute-start.2 = (bf16[4,3,24,512]{3,2,1,0:T(8,128)(2,1)S(1)}, bf16[4,3,24,512]{3,2,1,0:T(8,128)(2,1)S(1)}, u32[]{:S(2)}, u32[]{:S(2)}) collective-permute-start(bf16[4,3,24,512]{3,2,1,0:T(8,128)(2,1)S(1)} %get-tuple-element.23), channel_id=1, source_target_pairs={{0,112},{16,0},{32,16},{48,32},{64,48},{80,64},{96,80},{112,96},{1... | collective-permute-start | bytes 884744 | tf_op jit(solution)/shard_map/ppermute | solution.py:179
  19.7 8.9 %collective-permute-start.1 = (bf16[4,6,6,512]{3,2,1,0:T(8,128)(2,1)S(1)}, bf16[4,6,6,512]{3,2,1,0:T(8,128)(2,1)S(1)}, u32[]{:S(2)}, u32[]{:S(2)}) collective-permute-start(bf16[4,6,6,512]{3,2,1,0:T(8,128)(2,1)S(1)} %pad_maximum_fusion.5), channel_id=1, source_target_pairs={{0,15},{1,0},{2,1},{3,2},{4,3},{5,4},{6,5},{7,6},{8,7},{9,8},{10,9... | collective-permute-start | bytes 442376 | tf_op jit(solution)/shard_map/ppermute | solution.py:179
  26.7 6.2 %collective-permute-start.3 = (bf16[4,6,6,512]{3,2,1,0:T(8,128)(2,1)}, bf16[4,6,6,512]{3,2,1,0:T(8,128)(2,1)S(1)}, u32[]{:S(2)}, u32[]{:S(2)}) collective-permute-start(bf16[4,6,6,512]{3,2,1,0:T(8,128)(2,1)} %pad_maximum_fusion.4), channel_id=1, source_target_pairs={{0,15},{1,0},{2,1},{3,2},{4,3},{5,4},{6,5},{7,6},{8,7},{9,8},{10,9... | collective-permute-start | bytes 442376 | tf_op jit(solution)/shard_map/ppermute | solution.py:179
  57.0 1.1 copy-start.4
  59.4 1.1 copy-start.3
  60.1 5.7 %collective-permute-start.4 = (bf16[4,6,6,512]{3,0,2,1:T(4,128)(2,1)S(1)}, bf16[4,6,6,512]{3,0,2,1:T(4,128)(2,1)S(1)}, u32[]{:S(2)}, u32[]{:S(2)}) collective-permute-start(bf16[4,6,6,512]{3,0,2,1:T(4,128)(2,1)S(1)} %pad_maximum_fusion.7), channel_id=1, source_target_pairs={{0,1},{1,2},{2,3},{3,4},{4,5},{5,6},{6,7},{7,8},{8,9},{9,10},{10,1... | collective-permute-start | bytes 442376 | tf_op jit(solution)/shard_map/ppermute | solution.py:179
  62.5 5.6 %collective-permute-start.6 = (bf16[4,6,6,512]{3,0,2,1:T(4,128)(2,1)S(1)}, bf16[4,6,6,512]{3,0,2,1:T(4,128)(2,1)S(1)}, u32[]{:S(2)}, u32[]{:S(2)}) collective-permute-start(bf16[4,6,6,512]{3,0,2,1:T(4,128)(2,1)S(1)} %pad_maximum_fusion.6), channel_id=1, source_target_pairs={{0,1},{1,2},{2,3},{3,4},{4,5},{5,6},{6,7},{7,8},{8,9},{9,10},{10,1... | collective-permute-start | bytes 442376 | tf_op jit(solution)/shard_map/ppermute | solution.py:179
  66.6 12.0 %copy-start = (bf16[4,6,24,512]{3,2,1,0:T(8,128)(2,1)S(1)}, bf16[4,6,24,512]{3,2,1,0:T(8,128)(2,1)}, u32[]{:S(2)}) copy-start(bf16[4,6,24,512]{3,2,1,0:T(8,128)(2,1)} %param.4) | copy-start | bytes 1769476
  66.6 12.0 %collective-permute-start.5 = (bf16[4,3,24,512]{3,0,2,1:T(4,128)(2,1)S(1)}, bf16[4,3,24,512]{3,0,2,1:T(4,128)(2,1)S(1)}, u32[]{:S(2)}, u32[]{:S(2)}) collective-permute-start(bf16[4,3,24,512]{3,0,2,1:T(4,128)(2,1)S(1)} %get-tuple-element.20), channel_id=1, source_target_pairs={{0,16},{16,32},{32,48},{48,64},{64,80},{80,96},{96,112},{112,0},{1... | collective-permute-start | bytes 884744 | tf_op jit(solution)/shard_map/ppermute | solution.py:179
  68.8 17.7 %collective-permute-start.7 = (bf16[4,3,24,512]{3,0,2,1:T(4,128)(2,1)S(1)}, bf16[4,3,24,512]{3,0,2,1:T(4,128)(2,1)S(1)}, u32[]{:S(2)}, u32[]{:S(2)}) collective-permute-start(bf16[4,3,24,512]{3,0,2,1:T(4,128)(2,1)S(1)} %get-tuple-element.18), channel_id=1, source_target_pairs={{0,16},{16,32},{32,48},{48,64},{64,80},{80,96},{96,112},{112,0},{1... | collective-permute-start | bytes 884744 | tf_op jit(solution)/shard_map/ppermute | solution.py:179
  221.3 4.0 %copy-start.2 = (f32[512,512]{1,0:T(8,128)S(1)}, f32[512,512]{1,0:T(8,128)}, u32[]{:S(2)}) copy-start(f32[512,512]{1,0:T(8,128)} %get-tuple-element.17) | copy-start | bytes 3145732
Sparse Core Ops, SparseCore 0:
  57.2 164.0 all-reduce.2
where the time goes:
time: 233 us
  waiting for transfers between devices  164 us (70%)
  Pallas kernels  22.1 us (9%)
  between operations  14.3 us (6%)
  starting transfers between devices  12.3 us (5%)
  local copies, waits for them, and re-layouts  11.8 us (5%)
  other arithmetic  8.89 us (4%)
    psum x1, waiting for transfers between devices, body(): gqkv, gproj = lax.psum((gqkv, gproj), ('lat', 'lon'))  133 us
    ppermute x8, waiting for transfers between devices, shifted(): return lax.ppermute(value, axis, pairs)  30.5 us
    pallas_call x1, Pallas kernels, local_block(): pl.pallas_call(kernel, out_shape=(jax.ShapeDtypeStruct((4, 144, 512), BF)...  22.1 us
    ppermute x8, starting transfers between devices, shifted(): return lax.ppermute(value, axis, pairs)  12.2 us
    mul x2, other arithmetic, body(): return (output, grad_tokens, gqkv * norm, gproj * norm)  5.04 us
  transfers between devices with their start and end apart: 9, of which 8 were waited for; matrix products, arithmetic and copies ran while one was open for 5% of the time, Pallas kernels for 0%

commit v1 on v0

--- a/solution.py
+++ b/solution.py
@@ -170,6 +170,135 @@
         compiler_params=pltpu.CompilerParams(vmem_limit_bytes=56 * 2**20),
         name="window_block",
     )(tok, cot.reshape(576, 512), w_qkv, w_proj)
+MESH = pl.DeviceIdType.MESH
+NORM = 1.0 / 73728**0.5
+
+
+def place():
+    lat, lon = lax.axis_index("lat"), lax.axis_index("lon")
+    return lat * 8 + lon // 2, lon % 2
+
+
+def device(chip, core):
+    return chip // 8, (chip % 8) * 2 + core
+
+
+def drain(ref, sem):
+    pltpu.make_async_copy(ref, ref, sem).wait()
+
+
+def greet():
+    chip, core = place()
+    barrier = pltpu.get_barrier_semaphore()
+    pl.semaphore_signal(barrier, inc=1, device_id=device(chip, 1 - core), device_id_type=MESH)
+
+    @pl.loop(1, 64)
+    def _(t):
+        pl.semaphore_signal(barrier, inc=1, device_id=device(chip ^ t, core), device_id_type=MESH)
+
+    pl.semaphore_wait(barrier, 64)
+
+
+def core_swap(src, dst, send, recv):
+    chip, core = place()
+    return pltpu.make_async_remote_copy(
+        src_ref=src, dst_ref=dst, send_sem=send, recv_sem=recv,
+        device_id=device(chip, 1 - core), device_id_type=MESH,
+    )
+
+
+def scatter_start(mixed, parts, send, recv):
+    chip, core = place()
+
+    @pl.loop(1, 64)
+    def _(t):
+        pltpu.make_async_remote_copy(
+            src_ref=mixed.at[chip ^ t], dst_ref=parts.at[chip], send_sem=send, recv_sem=recv,
+            device_id=device(chip ^ t, core), device_id_type=MESH,
+        ).start()
+
+
+def gather_start(total, send, recv):
+    chip, core = place()
+
+    @pl.loop(1, 64)
+    def _(t):
+        pltpu.make_async_remote_copy(
+            src_ref=total.at[core, chip], dst_ref=total.at[core, chip], send_sem=send, recv_sem=recv,
+            device_id=device(chip ^ t, core), device_id_type=MESH,
+        ).start()
+
+
+def sum_kernel(grad_in, gqkv, gproj, grad, swapped, mixed, parts, total, send, recv):
+    chip, core = place()
+    greet()
+    for g in range(2):
+        grad[g] = grad_in[g]
+        swap = core_swap(grad.at[g, 1 - core], swapped.at[g], send.at[g, 0], recv.at[g, 0])
+        swap.start()
+        swap.wait()
+        mixed[g] = (grad[g, core].astype(F32) + swapped[g].astype(F32)).astype(BF)
+        scatter_start(mixed.at[g], parts.at[g], send.at[g, 1], recv.at[g, 1])
+        parts[g, chip] = mixed[g, chip]
+    for g in range(2):
+        drain(parts.at[g, pl.ds(0, 63)], recv.at[g, 1])
+        acc = jnp.sum(parts[g].astype(F32), axis=0) * NORM
+        total[g, core, chip] = acc.astype(BF)
+        gather_start(total.at[g], send.at[g, 2], recv.at[g, 2])
+    for g in range(2):
+        drain(parts.at[g, pl.ds(0, 63)], recv.at[g, 2])
+        swap = core_swap(total.at[g, core], total.at[g, core], send.at[g, 3], recv.at[g, 3])
+        swap.start()
+        swap.wait()
+        for part in range(3):
+            at = 512 * part + 256 * g
+            gqkv[:, at : at + 256] = rows_of(total, g, 512 * part, 512)
+        for half in range(2):
+            gproj[256 * g : 256 * g + 256, 256 * half : 256 * half + 256] = rows_of(total, g, 1536 + 256 * half, 256)
+        for i in range(1, 3):
+            drain(parts.at[g, pl.ds(0, 63)], send.at[g, i])
+
+
+def rows_of(total, g, start, count):
+    first, n = start // 16, count // 16
+    pieces = []
+    for half in range(2):
+        lo, hi = max(first, 64 * half), min(first + n, 64 * half + 64)
+        if lo < hi:
+            pieces.append(total[g, half, lo - 64 * half : hi - 64 * half].reshape(-1, 256))
+    return jnp.concatenate(pieces, axis=0).astype(F32)
+
+
+def sum_over_devices(gqkv, gproj):
+    halves = []
+    for g in range(2):
+        at = slice(256 * g, 256 * g + 256)
+        halves.append(jnp.concatenate(
+            [gqkv[:, 512 * part :][:, at] for part in range(3)] + [gproj[at, :256], gproj[at, 256:]], axis=0
+        ).astype(BF))
+    grad = jnp.stack(halves).reshape(2, 2, 64, 16, 256)
+    vm = pl.BlockSpec(memory_space=pltpu.VMEM)
+    return pl.pallas_call(
+        sum_kernel,
+        out_shape=(jax.ShapeDtypeStruct((512, 1536), F32), jax.ShapeDtypeStruct((512, 512), F32)),
+        in_specs=[vm],
+        out_specs=(vm, vm),
+        scratch_shapes=[
+            pltpu.VMEM((2, 2, 64, 16, 256), BF),
+            pltpu.VMEM((2, 64, 16, 256), BF),
+            pltpu.VMEM((2, 64, 16, 256), BF),
+            pltpu.VMEM((2, 64, 16, 256), BF),
+            pltpu.VMEM((2, 2, 64, 16, 256), BF),
+            pltpu.SemaphoreType.DMA((2, 4)),
+            pltpu.SemaphoreType.DMA((2, 4)),
+        ],
+        compiler_params=pltpu.CompilerParams(
+            vmem_limit_bytes=56 * 2**20, collective_id=0, has_side_effects=True
+        ),
+        name="sum_gradients",
+    )(grad)
+
+
 from jax.sharding import PartitionSpec as P
 
 
@@ -210,9 +339,8 @@
     dflat = roll_out(from_windows(dflat, 4, 6, 24))
     output = (tokens.astype(F32) + att.astype(F32)).astype(BF)
     grad_tokens = (cotangent.astype(F32) + dflat.astype(F32)).astype(BF)
-    gqkv, gproj = lax.psum((gqkv, gproj), ("lat", "lon"))
-    norm = 1.0 / 73728**0.5
-    return (output, grad_tokens, gqkv * norm, gproj * norm)
+    gqkv, gproj = sum_over_devices(gqkv, gproj)
+    return (output, grad_tokens, gqkv, gproj)
 
 
 def solution(mesh):

time: 233 us -> 122 us (0.52)
  waiting for transfers between devices: 164 us -> 11.6 us
  Pallas kernels: 22.1 us -> 73.1 us
  between operations: 14.3 us -> 0.99 us
  local copies, waits for them, and re-layouts: 11.8 us -> 16.2 us
    psum x1 -> x0, waiting for transfers between devices: 133 us -> none  [body(): gqkv, gproj = lax.psum((gqkv, gproj), ('lat', 'lon'))]
    pallas_call x0 -> x1, Pallas kernels: none -> 50.9 us  [sum_over_devices(): pl.pallas_call(sum_kernel, out_shape=(jax.ShapeDtypeStruct((512, 1536), F...]
    ppermute x8, waiting for transfers between devices: 30.5 us -> 11.6 us  [shifted(): return lax.ppermute(value, axis, pairs)]
    mul x2 -> x0, other arithmetic: 5.04 us -> none  [body(): return (output, grad_tokens, gqkv * norm, gproj * norm)]
    another operation x0 -> x3, other arithmetic: none -> 4.42 us
    unnamed x12 -> x22, local copies, waits for them, and re-layouts: 2.96 us -> 6.31 us
  transfers between devices with their start and end apart: 9 -> 8, of which waited for: 8 -> 4; matrix products, arithmetic and copies ran while one was open for 5% -> 10% of each run, Pallas kernels for 0% -> 42%
where the time goes in v1:
time: 122 us
  Pallas kernels  73.1 us (60%)
  local copies, waits for them, and re-layouts  16.2 us (13%)
  starting transfers between devices  11.8 us (10%)
  waiting for transfers between devices  11.6 us (10%)
  other arithmetic  8.24 us (7%)
    pallas_call x1, Pallas kernels, sum_over_devices(): pl.pallas_call(sum_kernel, out_shape=(jax.ShapeDtypeStruct((512, 1536), F...  50.9 us
    pallas_call x1, Pallas kernels, local_block(): pl.pallas_call(kernel, out_shape=(jax.ShapeDtypeStruct((4, 144, 512), BF)...  22.1 us
    ppermute x8, starting transfers between devices, shifted(): return lax.ppermute(value, axis, pairs)  11.8 us
    ppermute x8, waiting for transfers between devices, shifted(): return lax.ppermute(value, axis, pairs)  11.6 us
    unnamed x22, local copies, waits for them, and re-layouts  6.31 us
    another operation x2, other arithmetic  2.92 us
  transfers between devices with their start and end apart: 8, of which 4 were waited for; matrix products, arithmetic and copies ran while one was open for 10% of the time, Pallas kernels for 42%

profile of v1, /device:TPU:1, one launch (start us, length us, event | category | flops | bytes accessed | tf_op | source)
XLA Modules:
  0.0 122.0 jit_solution(9295912691062101382)
XLA Ops:
  0.6 1.2 fusion.19
  1.8 5.7 %collective-permute-start = (bf16[4,3,24,512]{3,2,1,0:T(8,128)(2,1)S(1)}, bf16[4,3,24,512]{3,2,1,0:T(8,128)(2,1)S(1)}, u32[]{:S(2)}, u32[]{:S(2)}) collective-permute-start(bf16[4,3,24,512]{3,2,1,0:T(8,128)(2,1)S(1)} %get-tuple-element.33), channel_id=1, source_target_pairs={{0,112},{16,0},{32,16},{48,32},{64,48},{80,64},{96,80},{112,96},{1... | collective-permute-start | bytes 884744 | tf_op jit(solution)/shard_map/ppermute | solution.py:308
  7.5 0.2 collective-permute-start.2
  7.8 5.4 %collective-permute-done = bf16[4,3,24,512]{3,2,1,0:T(8,128)(2,1)S(1)} collective-permute-done((bf16[4,3,24,512]{3,2,1,0:T(8,128)(2,1)S(1)}, bf16[4,3,24,512]{3,2,1,0:T(8,128)(2,1)S(1)}, u32[]{:S(2)}, u32[]{:S(2)}) %collective-permute-start) | collective-permute-done | bytes 294944 | tf_op jit(solution)/shard_map/ppermute | solution.py:308
  13.2 2.8 %collective-permute-start.1 = (bf16[4,6,6,512]{3,2,1,0:T(8,128)(2,1)S(1)}, bf16[4,6,6,512]{3,2,1,0:T(8,128)(2,1)S(1)}, u32[]{:S(2)}, u32[]{:S(2)}) collective-permute-start(bf16[4,6,6,512]{3,2,1,0:T(8,128)(2,1)S(1)} %pad_maximum_fusion.6), channel_id=1, source_target_pairs={{0,15},{1,0},{2,1},{3,2},{4,3},{5,4},{6,5},{7,6},{8,7},{9,8},{10,9... | collective-permute-start | bytes 442376 | tf_op jit(solution)/shard_map/ppermute | solution.py:308
  15.9 3.5 %collective-permute-done.2 = bf16[4,3,24,512]{3,2,1,0:T(8,128)(2,1)S(1)} collective-permute-done((bf16[4,3,24,512]{3,2,1,0:T(8,128)(2,1)S(1)}, bf16[4,3,24,512]{3,2,1,0:T(8,128)(2,1)S(1)}, u32[]{:S(2)}, u32[]{:S(2)}) %collective-permute-start.2) | collective-permute-done | bytes 294944 | tf_op jit(solution)/shard_map/ppermute | solution.py:308
  19.5 0.7 pad_maximum_fusion.5
  20.2 1.5 %collective-permute-start.3 = (bf16[4,6,6,512]{3,2,1,0:T(8,128)(2,1)}, bf16[4,6,6,512]{3,2,1,0:T(8,128)(2,1)S(1)}, u32[]{:S(2)}, u32[]{:S(2)}) collective-permute-start(bf16[4,6,6,512]{3,2,1,0:T(8,128)(2,1)} %pad_maximum_fusion.5), channel_id=1, source_target_pairs={{0,15},{1,0},{2,1},{3,2},{4,3},{5,4},{6,5},{7,6},{8,7},{9,8},{10,9... | collective-permute-start | bytes 442376 | tf_op jit(solution)/shard_map/ppermute | solution.py:308
  21.7 0.2 slice_maximum_fusion.1
  21.9 0.2 slice_maximum_fusion
  22.0 0.0 collective-permute-done.1
  22.0 0.1 fusion.5
  22.1 0.1 fusion.3
  22.2 0.5 copy.13
  22.7 0.2 reshape.74
  22.9 0.1 copy.25
  23.0 0.9 reshape.81.tok
  24.0 2.4 %collective-permute-done.3 = bf16[4,6,6,512]{3,2,1,0:T(8,128)(2,1)S(1)} collective-permute-done((bf16[4,6,6,512]{3,2,1,0:T(8,128)(2,1)}, bf16[4,6,6,512]{3,2,1,0:T(8,128)(2,1)S(1)}, u32[]{:S(2)}, u32[]{:S(2)}) %collective-permute-start.3) | collective-permute-done | bytes 147488 | tf_op jit(solution)/shard_map/ppermute | solution.py:308
  26.4 0.1 fusion.4
  26.4 0.1 fusion.2
  26.5 0.5 copy.15
  27.0 0.2 reshape.76
  27.2 0.1 copy.16
  27.4 0.9 reshape_reshape.3.cot
  28.3 22.1 %window_block.1 = (bf16[4,144,512]{2,1,0:T(8,128)(2,1)}, bf16[4,144,512]{2,1,0:T(8,128)(2,1)}, f32[512,1536]{1,0:T(8,128)}, f32[512,512]{1,0:T(8,128)}) custom-call(bf16[4,144,512]{2,1,0:T(8,128)(2,1)} %reshape.81.tok, bf16[576,512]{1,0:T(8,128)(2,1)} %reshape_reshape.3.cot, bf16[512,1536]{1,0:T(8,128)(2,1)} %w_qkv.1, bf16[512,512]{1,0:T(8,128)(2,1)} %w_proj.1), custom_call_target="tpu_custom_call" | custom-call | tf_op jit(solution)/shard_map/window_block/pallas_call | solution.py:143
  50.4 1.5 %copy.18 = bf16[4,144,512]{2,0,1:T(4,128)(2,1)S(1)} copy(bf16[4,144,512]{2,1,0:T(8,128)(2,1)} %get-tuple-element.10) | data formatting | bytes 1179648 | tf_op jit(solution)/shard_map/window_block/pallas_call | solution.py:143
  51.9 0.2 reshape.77
  52.2 0.6 copy.19
  52.8 0.2 reshape.78
  53.0 0.0 copy-start.4
  53.0 0.3 slice.166
  53.4 0.2 pad_maximum_fusion.8
  53.5 0.3 collective-permute-start.4
  53.8 0.4 copy-done.4
  54.2 0.9 convert.35
  55.1 0.5 copy.21
  55.6 0.2 reshape.79
  55.8 0.6 copy.22
  56.4 0.2 reshape.80
  56.6 0.3 slice.170
  57.0 0.2 pad_maximum_fusion.7
  57.1 1.2 %collective-permute-start.6 = (bf16[4,6,6,512]{3,0,2,1:T(4,128)(2,1)S(1)}, bf16[4,6,6,512]{3,0,2,1:T(4,128)(2,1)S(1)}, u32[]{:S(2)}, u32[]{:S(2)}) collective-permute-start(bf16[4,6,6,512]{3,0,2,1:T(4,128)(2,1)S(1)} %pad_maximum_fusion.7), channel_id=1, source_target_pairs={{0,1},{1,2},{2,3},{3,4},{4,5},{5,6},{6,7},{7,8},{8,9},{9,10},{10,1... | collective-permute-start | bytes 442376 | tf_op jit(solution)/shard_map/ppermute | solution.py:308
  58.4 2.1 %convert.34 = bf16[512,1536]{1,0:T(8,128)(2,1)S(1)} convert(f32[512,1536]{1,0:T(8,128)} %get-tuple-element.12) | non-fusion elementwise | flops 786432 | bytes 4718592 | tf_op jit(solution)/shard_map/convert.29
  60.5 0.0 copy-start.3
  60.6 0.9 copy-done.3
  61.6 0.0 collective-permute-done.4
  61.6 0.5 fusion.1
  62.1 0.2 fusion.17
  62.3 0.1 collective-permute-start.5
  62.4 0.3 collective-permute-done.6
  62.7 0.5 fusion
  63.2 0.2 fusion.16
  63.5 0.1 collective-permute-start.7
  63.5 1.5 %pad_maximum_fusion.grad_in = bf16[2,2,64,16,256]{4,3,2,1,0:T(8,128)(2,1)} fusion(bf16[1,2,64,16,256]{4,3,2,1,0:T(8,128)(2,1)S(1)} %bitcast.73, bf16[1,2,64,16,256]{4,3,2,1,0:T(8,128)(2,1)S(1)} %bitcast.72), kind=kLoop, calls=%fused_computation | loop fusion | flops 1048576 | bytes 4194304 | tf_op jit(solution)/shard_map/stack | solution.py:279
  65.0 50.9 %sum_gradients.1 = (f32[512,1536]{1,0:T(8,128)}, f32[512,512]{1,0:T(8,128)}) custom-call(bf16[2,2,64,16,256]{4,3,2,1,0:T(8,128)(2,1)} %pad_maximum_fusion.grad_in), custom_call_target="tpu_custom_call" | custom-call | tf_op jit(solution)/shard_map/sum_gradients/pallas_call | solution.py:281
  116.0 0.0 collective-permute-done.5
  116.0 0.6 add_convert_fusion.1
  116.6 0.9 copy.23
  117.5 0.0 collective-permute-done.7
  117.5 0.6 add_convert_fusion
  118.1 0.9 copy.24
  119.1 1.7 %copy.39 = f32[512,1536]{1,0:T(8,128)} copy(f32[512,1536]{1,0:T(8,128)S(1)} %copy-done) | data formatting | bytes 6291456
  120.7 0.3 copy-done.5
  121.0 1.0 copy.40
  (16 shorter events, 0.2 us)
Async XLA Ops:
  0.6 6.8 %copy-start.2 = (bf16[4,6,24,512]{3,2,1,0:T(8,128)(2,1)S(1)}, bf16[4,6,24,512]{3,2,1,0:T(8,128)(2,1)}, u32[]{:S(2)}) copy-start(bf16[4,6,24,512]{3,2,1,0:T(8,128)(2,1)} %param.5) | copy-start | bytes 1769476
  1.8 11.3 %collective-permute-start = (bf16[4,3,24,512]{3,2,1,0:T(8,128)(2,1)S(1)}, bf16[4,3,24,512]{3,2,1,0:T(8,128)(2,1)S(1)}, u32[]{:S(2)}, u32[]{:S(2)}) collective-permute-start(bf16[4,3,24,512]{3,2,1,0:T(8,128)(2,1)S(1)} %get-tuple-element.33), channel_id=1, source_target_pairs={{0,112},{16,0},{32,16},{48,32},{64,48},{80,64},{96,80},{112,96},{1... | collective-permute-start | bytes 884744 | tf_op jit(solution)/shard_map/ppermute | solution.py:308
  7.5 12.0 %collective-permute-start.2 = (bf16[4,3,24,512]{3,2,1,0:T(8,128)(2,1)S(1)}, bf16[4,3,24,512]{3,2,1,0:T(8,128)(2,1)S(1)}, u32[]{:S(2)}, u32[]{:S(2)}) collective-permute-start(bf16[4,3,24,512]{3,2,1,0:T(8,128)(2,1)S(1)} %get-tuple-element.31), channel_id=1, source_target_pairs={{0,112},{16,0},{32,16},{48,32},{64,48},{80,64},{96,80},{112,96},{1... | collective-permute-start | bytes 884744 | tf_op jit(solution)/shard_map/ppermute | solution.py:308
  13.2 8.9 %collective-permute-start.1 = (bf16[4,6,6,512]{3,2,1,0:T(8,128)(2,1)S(1)}, bf16[4,6,6,512]{3,2,1,0:T(8,128)(2,1)S(1)}, u32[]{:S(2)}, u32[]{:S(2)}) collective-permute-start(bf16[4,6,6,512]{3,2,1,0:T(8,128)(2,1)S(1)} %pad_maximum_fusion.6), channel_id=1, source_target_pairs={{0,15},{1,0},{2,1},{3,2},{4,3},{5,4},{6,5},{7,6},{8,7},{9,8},{10,9... | collective-permute-start | bytes 442376 | tf_op jit(solution)/shard_map/ppermute | solution.py:308
  20.2 6.2 %collective-permute-start.3 = (bf16[4,6,6,512]{3,2,1,0:T(8,128)(2,1)}, bf16[4,6,6,512]{3,2,1,0:T(8,128)(2,1)S(1)}, u32[]{:S(2)}, u32[]{:S(2)}) collective-permute-start(bf16[4,6,6,512]{3,2,1,0:T(8,128)(2,1)} %pad_maximum_fusion.5), channel_id=1, source_target_pairs={{0,15},{1,0},{2,1},{3,2},{4,3},{5,4},{6,5},{7,6},{8,7},{9,8},{10,9... | collective-permute-start | bytes 442376 | tf_op jit(solution)/shard_map/ppermute | solution.py:308
  53.0 1.2 %copy-start.4 = (f32[512,512]{1,0:T(8,128)S(1)}, f32[512,512]{1,0:T(8,128)}, u32[]{:S(2)}) copy-start(f32[512,512]{1,0:T(8,128)} %get-tuple-element.13) | copy-start | bytes 3145732
  53.4 1.8 %copy-start.6 = (bf16[4,144,512]{2,1,0:T(8,128)(2,1)S(1)}, bf16[4,144,512]{2,1,0:T(8,128)(2,1)}, u32[]{:S(2)}) copy-start(bf16[4,144,512]{2,1,0:T(8,128)(2,1)} %get-tuple-element.11) | copy-start | bytes 1769476
  53.5 8.0 %collective-permute-start.4 = (bf16[4,6,6,512]{3,0,2,1:T(4,128)(2,1)S(1)}, bf16[4,6,6,512]{3,0,2,1:T(4,128)(2,1)S(1)}, u32[]{:S(2)}, u32[]{:S(2)}) collective-permute-start(bf16[4,6,6,512]{3,0,2,1:T(4,128)(2,1)S(1)} %pad_maximum_fusion.8), channel_id=1, source_target_pairs={{0,1},{1,2},{2,3},{3,4},{4,5},{5,6},{6,7},{7,8},{8,9},{9,10},{10,1... | collective-permute-start | bytes 442376 | tf_op jit(solution)/shard_map/ppermute | solution.py:308
  57.1 5.6 %collective-permute-start.6 = (bf16[4,6,6,512]{3,0,2,1:T(4,128)(2,1)S(1)}, bf16[4,6,6,512]{3,0,2,1:T(4,128)(2,1)S(1)}, u32[]{:S(2)}, u32[]{:S(2)}) collective-permute-start(bf16[4,6,6,512]{3,0,2,1:T(4,128)(2,1)S(1)} %pad_maximum_fusion.7), channel_id=1, source_target_pairs={{0,1},{1,2},{2,3},{3,4},{4,5},{5,6},{6,7},{7,8},{8,9},{9,10},{10,1... | collective-permute-start | bytes 442376 | tf_op jit(solution)/shard_map/ppermute | solution.py:308
  60.5 1.0 copy-start.3
  62.3 53.7 %collective-permute-start.5 = (bf16[4,3,24,512]{3,0,2,1:T(4,128)(2,1)S(1)}, bf16[4,3,24,512]{3,0,2,1:T(4,128)(2,1)S(1)}, u32[]{:S(2)}, u32[]{:S(2)}) collective-permute-start(bf16[4,3,24,512]{3,0,2,1:T(4,128)(2,1)S(1)} %get-tuple-element.28), channel_id=1, source_target_pairs={{0,16},{16,32},{32,48},{48,64},{64,80},{80,96},{96,112},{112,0},{1... | collective-permute-start | bytes 884744 | tf_op jit(solution)/shard_map/ppermute | solution.py:308
  63.5 54.1 %collective-permute-start.7 = (bf16[4,3,24,512]{3,0,2,1:T(4,128)(2,1)S(1)}, bf16[4,3,24,512]{3,0,2,1:T(4,128)(2,1)S(1)}, u32[]{:S(2)}, u32[]{:S(2)}) collective-permute-start(bf16[4,3,24,512]{3,0,2,1:T(4,128)(2,1)S(1)} %get-tuple-element.26), channel_id=1, source_target_pairs={{0,16},{16,32},{32,48},{48,64},{64,80},{80,96},{96,112},{112,0},{1... | collective-permute-start | bytes 884744 | tf_op jit(solution)/shard_map/ppermute | solution.py:308
  65.0 51.0 %copy-start.1 = (bf16[4,6,24,512]{3,2,1,0:T(8,128)(2,1)S(1)}, bf16[4,6,24,512]{3,2,1,0:T(8,128)(2,1)}, u32[]{:S(2)}) copy-start(bf16[4,6,24,512]{3,2,1,0:T(8,128)(2,1)} %param.4) | copy-start | bytes 1769476
  116.6 2.4 %copy-start = (f32[512,1536]{1,0:T(8,128)S(1)}, f32[512,1536]{1,0:T(8,128)}, u32[]{:S(2)}) copy-start(f32[512,1536]{1,0:T(8,128)} %get-tuple-element.44) | copy-start | bytes 9437188
  119.1 2.0 %copy-start.5 = (f32[512,512]{1,0:T(8,128)S(1)}, f32[512,512]{1,0:T(8,128)}, u32[]{:S(2)}) copy-start(f32[512,512]{1,0:T(8,128)} %get-tuple-element.45) | copy-start | bytes 3145732

commit v2 on v0

v2 whole, which is shorter than its diff:
```python
import numpy as np
import jax
import jax.numpy as jnp
from jax import lax
from jax.experimental import pallas as pl
from jax.experimental.pallas import tpu as pltpu
from jax.sharding import PartitionSpec as P

BF = jnp.bfloat16
F32 = jnp.float32
SCALE = 1.0 / 32**0.5
EXP2 = SCALE * 1.4426950408889634
NORM = 1.0 / 73728**0.5
NN = (((1,), (0,)), ((), ()))
NT = (((1,), (1,)), ((), ()))
TN = (((0,), (0,)), ((), ()))
MESH = pl.DeviceIdType.MESH

STARTS = (0, 224, 448, 528)
ROWS = 608
SECTIONS = ((224, 224), (448, 80), (528, 80))


def section_row(array, level, row, col):
    section = (2 if col < 6 else 0) + (1 if row < 3 else 0)
    width, first = (18, 6) if col >= 6 else (6, 0)
    at = (level * 3 + row % 3) * width + col - first
    return STARTS[section] + array * 6 * width + at


def orders():
    pack = np.zeros((ROWS, 576), np.float32)
    place = np.zeros((576, ROWS), np.float32)
    for array in range(2):
        for level in range(2):
            for row in range(6):
                for col in range(24):
                    at = array * 288 + level * 144 + row * 24 + col
                    pack[section_row(array, level, row, col), at] = 1
            for row in range(6):
                for col in range(24):
                    at = array * 288 + col // 12 * 144 + level * 72 + row * 12 + col % 12
                    source = section_row(array, level, (row + 3) % 6, (col + 6) % 24)
                    place[at, source] = 1
    return [jnp.asarray(m, BF) for m in (pack, place, place.T, pack.T)]


def dot(a, b, dims=NN):
    return lax.dot_general(a, b, dims, preferred_element_type=F32)


def head_mask(dtype):
    head = lax.broadcasted_iota(jnp.int32, (128, 256), 0) >> 4
    col = lax.broadcasted_iota(jnp.int32, (128, 256), 1) >> 5
    return (head == col).astype(dtype)


def window_rows(w):
    return pl.ds(pl.multiple_of(w * 144, 16), 144)


def project(w, tok, cot, w_qkv, w_proj, hat, normed, inv, q, k, v, dc):
    x = tok[window_rows(w), :].astype(F32)
    x = x - jnp.mean(x, axis=1, keepdims=True)
    scale = lax.rsqrt(jnp.mean(x * x, axis=1, keepdims=True) + 1e-05)
    x = x * scale
    hat[w] = x
    inv[w] = jnp.broadcast_to(scale, (144, 128))
    x = x.astype(BF)
    rows = window_rows(w)
    normed[rows, :] = x
    for part, ref in enumerate((q, k, v)):
        for g in range(2):
            at = 512 * part + 256 * g
            ref[g, w] = dot(x, w_qkv[:, at : at + 256]).astype(BF)
    c = cot[rows, :]
    for g in range(2):
        dc[g, w] = dot(c, w_proj[256 * g : 256 * g + 256, :], NT).astype(BF)


def attend(g, w, lat_last, lon_last, mask, maskf, q, k, v, dc, qs, cs, pt, st, sf, df, ctx, dqkv):
    klab, qlab = labels(w, lat_last, lon_last)
    keys = k[g, w]
    vals = v[g, w]
    rows = window_rows(w)
    for c in range(9):
        at = slice(128 * c, 128 * c + 128)
        q16 = q[g, w, 16 * c : 16 * c + 16, :]
        d16 = dc[g, w, 16 * c : 16 * c + 16, :]
        qs[at, :] = jnp.concatenate([q16] * 8, axis=0) * mask
        cs[at, :] = jnp.concatenate([d16] * 8, axis=0) * mask
    sf[...] = dot(keys, qs[...], NT)
    df[...] = dot(vals, cs[...], NT)
    for c in range(9):
        at = slice(128 * c, 128 * c + 128)
        s = sf[:, at]
        s = jnp.where(klab == qlab[c], s, -1e30)
        e = jnp.exp2((s - jnp.max(s, axis=0, keepdims=True)) * EXP2)
        p = e * (1.0 / jnp.sum(e, axis=0, keepdims=True))
        pt[:, at] = p.astype(BF)
        dp = df[:, at]
        inner = jnp.sum(p * dp, axis=0, keepdims=True)
        st[:, at] = ((p * SCALE) * (dp - inner)).astype(BF)
    out = dot(pt[...], vals, TN).reshape(9, 8, 16, 256) * maskf.reshape(1, 8, 16, 256)
    ctx[g, rows, :] = jnp.sum(out, axis=1).reshape(144, 256).astype(BF)
    out = dot(st[...], keys, TN).reshape(9, 8, 16, 256) * maskf.reshape(1, 8, 16, 256)
    dqkv[g, rows, 0:256] = jnp.sum(out, axis=1).reshape(144, 256).astype(BF)
    dqkv[g, rows, 256:512] = dot(st[...], qs[...]).astype(BF)
    dqkv[g, rows, 512:768] = dot(pt[...], cs[...]).astype(BF)


def finish(p, i, w_qkv, w_proj, hat, inv, ctx, dqkv, done):
    w = 2 * p + i
    rows = window_rows(w)
    a = dot(ctx[0, rows, :], w_proj[0:256, :]) + dot(ctx[1, rows, :], w_proj[256:512, :])
    done[p, window_rows(i), :] = a.astype(BF)
    d = None
    for g in range(2):
        for part in range(3):
            at = 512 * part + 256 * g
            t = dot(dqkv[g, rows, 256 * part : 256 * part + 256], w_qkv[:, at : at + 256], NT)
            d = t if d is None else d + t
    h = hat[w]
    d = d - jnp.mean(d, axis=1, keepdims=True) - h * jnp.mean(d * h, axis=1, keepdims=True)
    scale = jnp.concatenate([inv[w]] * 4, axis=1)
    done[p, window_rows(2 + i), :] = (d * scale).astype(BF)


def labels(w, lat_last, lon_last):
    def flags(t):
        level = (t >= 72).astype(jnp.int32)
        t = t - 72 * level
        row = (t >= 36).astype(jnp.int32)
        t = t - 36 * row
        t = jnp.where(t >= 24, t - 24, jnp.where(t >= 12, t - 12, t))
        col = (t >= 6).astype(jnp.int32)
        return level * is_b + row * lat_last + col * last

    is_b = 4 * (w // 2)
    last = lon_last * (w % 2)
    klab = flags(lax.broadcasted_iota(jnp.int32, (144, 128), 0))
    lane = lax.broadcasted_iota(jnp.int32, (1, 128), 1) & 15
    qlab = [flags(lane + 16 * c) for c in range(9)]
    return klab, qlab


def weight_gradients(g, normed, cot, ctx, dqkv, grad):
    for part in range(3):
        d = dot(normed[...], dqkv[g, :, 256 * part : 256 * part + 256], TN).astype(BF)
        at = 32 * (part % 2)
        grad[g, part // 2, at : at + 32] = d.reshape(32, 16, 256)
    for half in range(2):
        d = dot(ctx[g], cot[:, 256 * half : 256 * half + 256], TN).astype(BF)
        at = 32 + 16 * half
        grad[g, 1, at : at + 16] = d.reshape(16, 16, 256)


def place():
    lat, lon = lax.axis_index("lat"), lax.axis_index("lon")
    return lat * 8 + lon // 2, lon % 2


def device(chip, core):
    return chip // 8, (chip % 8) * 2 + core


def beside(lat_step, lon_step):
    lat, lon = lax.axis_index("lat"), lax.axis_index("lon")
    return lax.rem(lat + lat_step + 8, 8), lax.rem(lon + lon_step + 16, 16)


def drain(ref, sem):
    pltpu.make_async_copy(ref, ref, sem).wait()


def greet():
    chip, core = place()
    barrier = pltpu.get_barrier_semaphore()
    for steps in ((0, -1), (0, 1), (-1, -1), (1, 1)):
        pl.semaphore_signal(barrier, inc=1, device_id=beside(*steps), device_id_type=MESH)
    pl.semaphore_signal(barrier, inc=1, device_id=device(chip, 1 - core), device_id_type=MESH)

    @pl.loop(1, 64)
    def _(t):
        pl.semaphore_signal(barrier, inc=1, device_id=device(chip ^ t, core), device_id_type=MESH)


def meet():
    pl.semaphore_wait(pltpu.get_barrier_semaphore(), 68)


def halo(p, step, src, dst, send, recv):
    copies = []
    for s, (at, count) in enumerate(SECTIONS):
        lat_step, lon_step = ((step, 0), (0, step), (step, step))[s]
        copies.append(pltpu.make_async_remote_copy(
            src_ref=src.at[p, pl.ds(at, count)], dst_ref=dst.at[p, pl.ds(at, count)],
            send_sem=send.at[p, s], recv_sem=recv.at[p, s],
            device_id=beside(lat_step, lon_step), device_id_type=MESH,
        ))
    return copies


def core_swap(src, dst, send, recv):
    chip, core = place()
    return pltpu.make_async_remote_copy(
        src_ref=src, dst_ref=dst, send_sem=send, recv_sem=recv,
        device_id=device(chip, 1 - core), device_id_type=MESH,
    )


def scatter_start(mixed, parts, send, recv):
    chip, core = place()

    @pl.loop(1, 64)
    def _(t):
        pltpu.make_async_remote_copy(
            src_ref=mixed.at[chip ^ t], dst_ref=parts.at[chip], send_sem=send, recv_sem=recv,
            device_id=device(chip ^ t, core), device_id_type=MESH,
        ).start()


def gather_start(total, send, recv):
    chip, core = place()

    @pl.loop(1, 64)
    def _(t):
        pltpu.make_async_remote_copy(
            src_ref=total.at[core, chip], dst_ref=total.at[core, chip], send_sem=send, recv_sem=recv,
            device_id=device(chip ^ t, core), device_id_type=MESH,
        ).start()


def kernel(
    tokens, cotangent, w_qkv_in, w_proj_in, pack_in, place_in, unplace_in, unpack_in,
    att, dflat, total,
    both, w_qkv, w_proj, pack, place_m, unplace, unpack, out_halo, in_halo, out_back, in_back,
    tok, cot, hat, normed, inv, q, k, v, dc, qs, cs, pt, st, sf, df, ctx, dqkv, done,
    grad, swapped, mixed, parts, load, send, recv, hsend, hrecv, bsend, brecv,
):
    chip, core = place()
    greet()
    loads = []

    def fetch(src, dst):
        copy = pltpu.make_async_copy(src, dst, load.at[len(loads)])
        copy.start()
        loads.append(copy)

    for p in range(2):
        for half, src in enumerate((tokens, cotangent)):
            for level in range(2):
                fetch(
                    src.at[pl.ds(144 * ((2 * p + 1 + level) % 4), 144)],
                    both.at[p, pl.ds(288 * half + 144 * level, 144)],
                )
    fetch(pack_in, pack)
    early = len(loads)
    fetch(place_in, place_m)
    fetch(w_qkv_in, w_qkv)
    fetch(w_proj_in, w_proj)
    fetch(unplace_in, unplace)
    fetch(unpack_in, unpack)
    for copy in loads[:early]:
        copy.wait()
    out_halo[0] = dot(pack[...], both[0]).astype(BF)
    meet()
    coming = [halo(p, -1, out_halo, in_halo, hsend, hrecv) for p in range(2)]
    for copy in coming[0]:
        copy.start()
    out_halo[1] = dot(pack[...], both[1]).astype(BF)
    for copy in coming[1]:
        copy.start()
    for copy in loads[early:]:
        copy.wait()
    lat_last = 2 * (lax.axis_index("lat") == 7).astype(jnp.int32)
    lon_last = (lax.axis_index("lon") == 15).astype(jnp.int32)
    mask = head_mask(BF)
    maskf = head_mask(F32)

    def arrive(p):
        in_halo[p, 0:224] = out_halo[p, 0:224]
        for copy in coming[p]:
            copy.wait_recv()
        tok[288 * p : 288 * p + 288, :] = dot(place_m[0:288, :], in_halo[p]).astype(BF)
        cot[288 * p : 288 * p + 288, :] = dot(place_m[288:576, :], in_halo[p]).astype(BF)

        @pl.loop(2 * p, 2 * p + 2)
        def _(w):
            project(w, tok, cot, w_qkv, w_proj, hat, normed, inv, q, k, v, dc)

    def attention(g, w):
        attend(g, w, lat_last, lon_last, mask, maskf, q, k, v, dc, qs, cs, pt, st, sf, df, ctx, dqkv)

    def swap_in(g):
        return core_swap(grad.at[g, 1 - core], swapped.at[g], send.at[g, 0], recv.at[g, 0])

    def mix(g):
        swap_in(g).wait()
        mixed[g] = (grad[g, core].astype(F32) + swapped[g].astype(F32)).astype(BF)
        scatter_start(mixed.at[g], parts.at[g], send.at[g, 1], recv.at[g, 1])
        parts[g, chip] = mixed[g, chip]

    def leave(p):
        @pl.loop(0, 2)
        def _(i):
            finish(p, i, w_qkv, w_proj, hat, inv, ctx, dqkv, done)

        out_back[p] = dot(unplace[...], done[p]).astype(BF)
        for copy in going[p]:
            copy.start()

    going = [halo(p, 1, out_back, in_back, bsend, brecv) for p in range(2)]
    arrive(0)

    @pl.loop(0, 4)
    def _(i):
        attention(i // 2, i % 2)

    arrive(1)

    @pl.loop(0, 2)
    def _(g):
        @pl.loop(2, 4)
        def _(w):
            attention(g, w)

        weight_gradients(g, normed, cot, ctx, dqkv, grad)
        swap_in(g).start()

        @pl.when(g == 1)
        def _():
            mix(0)

    leave(0)
    mix(1)
    leave(1)
    for g in range(2):
        drain(parts.at[g, pl.ds(0, 63)], recv.at[g, 1])
        acc = jnp.sum(parts[g].astype(F32), axis=0) * NORM
        total[g, core, chip] = acc.astype(BF)
        gather_start(total.at[g], send.at[g, 2], recv.at[g, 2])
    for p in range(2):
        in_back[p, 0:224] = out_back[p, 0:224]
        for copy in going[p]:
            copy.wait_recv()
        for half, out in enumerate((att, dflat)):
            for level in range(2):
                at = 144 * ((2 * p + 1 + level) % 4)
                rows = slice(288 * half + 144 * level, 288 * half + 144 * level + 144)
                out[at : at + 144, :] = dot(unpack[rows, :], in_back[p]).astype(BF)
    swaps = []
    for g in range(2):
        drain(parts.at[g, pl.ds(0, 63)], recv.at[g, 2])
        swaps.append(core_swap(total.at[g, core], total.at[g, core], send.at[g, 3], recv.at[g, 3]))
        swaps[g].start()
    for g in range(2):
        swaps[g].wait()
        for i in range(1, 3):
            drain(parts.at[g, pl.ds(0, 63)], send.at[g, i])
    for p in range(2):
        for copy in coming[p] + going[p]:
            copy.wait_send()


def block(tokens, cotangent, w_qkv, w_proj):
    hbm = pl.BlockSpec(memory_space=pl.ANY)
    vm = pl.BlockSpec(memory_space=pltpu.VMEM)
    dma = pltpu.SemaphoreType.DMA
    return pl.pallas_call(
        kernel,
        out_shape=(
            jax.ShapeDtypeStruct((576, 512), BF),
            jax.ShapeDtypeStruct((576, 512), BF),
            jax.ShapeDtypeStruct((2, 2, 64, 16, 256), BF),
        ),
        in_specs=[hbm] * 8,
        out_specs=(vm,) * 3,
        scratch_shapes=[
            pltpu.VMEM((2, 576, 512), BF),
            pltpu.VMEM((512, 1536), BF),
            pltpu.VMEM((512, 512), BF),
            pltpu.VMEM((ROWS, 576), BF),
            pltpu.VMEM((576, ROWS), BF),
            pltpu.VMEM((ROWS, 576), BF),
            pltpu.VMEM((576, ROWS), BF),
            pltpu.VMEM((2, ROWS, 512), BF),
            pltpu.VMEM((2, ROWS, 512), BF),
            pltpu.VMEM((2, ROWS, 512), BF),
            pltpu.VMEM((2, ROWS, 512), BF),
            pltpu.VMEM((576, 512), BF),
            pltpu.VMEM((576, 512), BF),
            pltpu.VMEM((4, 144, 512), F32),
            pltpu.VMEM((576, 512), BF),
            pltpu.VMEM((4, 144, 128), F32),
            pltpu.VMEM((2, 4, 144, 256), BF),
            pltpu.VMEM((2, 4, 144, 256), BF),
            pltpu.VMEM((2, 4, 144, 256), BF),
            pltpu.VMEM((2, 4, 144, 256), BF),
            pltpu.VMEM((1152, 256), BF),
            pltpu.VMEM((1152, 256), BF),
            pltpu.VMEM((144, 1152), BF),
            pltpu.VMEM((144, 1152), BF),
            pltpu.VMEM((144, 1152), F32),
            pltpu.VMEM((144, 1152), F32),
            pltpu.VMEM((2, 576, 256), BF),
            pltpu.VMEM((2, 576, 768), BF),
            pltpu.VMEM((2, 576, 512), BF),
            pltpu.VMEM((2, 2, 64, 16, 256), BF),
            pltpu.VMEM((2, 64, 16, 256), BF),
            pltpu.VMEM((2, 64, 16, 256), BF),
            pltpu.VMEM((2, 64, 16, 256), BF),
            dma((16,)),
            dma((2, 4)),
            dma((2, 4)),
            dma((2, 3)),
            dma((2, 3)),
            dma((2, 3)),
            dma((2, 3)),
        ],
        compiler_params=pltpu.CompilerParams(
            vmem_limit_bytes=56 * 2**20, collective_id=0, has_side_effects=True
        ),
        name="window_block",
    )(tokens, cotangent, w_qkv, w_proj, *orders())


def body(tokens, cotangent, w_qkv, w_proj):
    shape = tokens.shape
    att, dflat, total = block(tokens.reshape(576, 512), cotangent.reshape(576, 512), w_qkv, w_proj)
    output = (tokens.astype(F32) + att.reshape(shape).astype(F32)).astype(BF)
    grad_tokens = (cotangent.astype(F32) + dflat.reshape(shape).astype(F32)).astype(BF)
    total = total.reshape(2, 2048, 256)
    gqkv = total[:, :1536].reshape(2, 3, 512, 256).transpose(2, 1, 0, 3).reshape(512, 1536)
    gproj = total[:, 1536:].reshape(2, 2, 256, 256).transpose(0, 2, 1, 3).reshape(512, 512)
    return (output, grad_tokens, gqkv.astype(F32), gproj.astype(F32))


def solution(mesh):
    spec = P(None, "lat", "lon", None)
    return jax.shard_map(
        body,
        mesh=mesh,
        in_specs=(spec, spec, P(), P()),
        out_specs=(spec, spec, P(), P()),
        check_vma=False,
    )
```

time: 233 us -> 92.5 us (0.40)
  waiting for transfers between devices: 164 us -> 0 us
  Pallas kernels: 22.1 us -> 81.9 us
  between operations: 14.3 us -> 0.7 us
  starting transfers between devices: 12.3 us -> 0 us
  other arithmetic: 8.89 us -> 2.74 us
  local copies, waits for them, and re-layouts: 11.8 us -> 7.04 us
    psum x1 -> x0, waiting for transfers between devices: 133 us -> none  [body(): gqkv, gproj = lax.psum((gqkv, gproj), ('lat', 'lon'))]
    pallas_call x1, Pallas kernels: 22.1 us -> 81.9 us  [block(): pl.pallas_call(kernel, out_shape=(jax.ShapeDtypeStruct((576, 512), BF), j...]
    ppermute x8 -> x0, waiting for transfers between devices: 30.5 us -> none  [shifted(): return lax.ppermute(value, axis, pairs)]
    ppermute x8 -> x0, starting transfers between devices: 12.2 us -> none  [shifted(): return lax.ppermute(value, axis, pairs)]
    convert_element_type x0 -> x3, local copies, waits for them, and re-layouts: none -> 5.85 us  [body(): return (output, grad_tokens, gqkv.astype(F32), gproj.astype(F32))]
    mul x2 -> x0, other arithmetic: 5.04 us -> none  [body(): return (output, grad_tokens, gqkv * norm, gproj * norm)]
    reshape x8 -> x0, local copies, waits for them, and re-layouts: 2.44 us -> none  [the longest x2 1.09 us: to_windows(): return field.transpose(0, 2, 4, 1, 3, 5, 6).reshape(-1, 144, width)]
  transfers between devices with their start and end apart: 9 -> 0, of which waited for: 8 -> 0; matrix products, arithmetic and copies ran while one was open for 5% -> 0% of each run, Pallas kernels for 0% -> 0%
where the time goes in v2:
time: 92.5 us; the launch traced here: 92.4 us
  Pallas kernels  81.9 us (89%)
  local copies, waits for them, and re-layouts  7.04 us (8%)
  other arithmetic  2.74 us (3%)
    pallas_call x1, Pallas kernels, block(): pl.pallas_call(kernel, out_shape=(jax.ShapeDtypeStruct((576, 512), BF), j...  81.9 us
    convert_element_type x3, local copies, waits for them, and re-layouts, body(): return (output, grad_tokens, gqkv.astype(F32), gproj.astype(F32))  5.85 us
    convert_element_type x1, other arithmetic, body(): (cotangent.astype(F32) + dflat.reshape(shape).astype(F32)).astype(BF)  2.74 us

profile of v2, /device:TPU:1, one launch (start us, length us, event | category | flops | bytes accessed | tf_op | source)
XLA Modules:
  0.0 92.4 jit_solution(2360288894330362433)
XLA Ops:
  0.6 0.0 copy-start
  0.6 0.0 copy-start.1
  0.7 81.9 %window_block.1 = (bf16[576,512]{1,0:T(8,128)(2,1)}, bf16[576,512]{1,0:T(8,128)(2,1)}, bf16[2,2,64,16,256]{4,3,2,1,0:T(8,128)(2,1)}) custom-call(bf16[576,512]{1,0:T(8,128)(2,1)} %bitcast.21, bf16[576,512]{1,0:T(8,128)(2,1)} %bitcast.22, bf16[512,1536]{1,0:T(8,128)(2,1)} %w_qkv_in.1, bf16[512,512]{1,0:T(8,128)(2,1)} %w_proj_in.1, ...), custom_call_target="tpu_custom_call" | custom-call | tf_op jit(solution)/shard_map/window_block/pallas_call | solution.py:370
  82.6 0.0 copy-done
  82.6 0.0 copy-done.1
  82.6 0.0 copy-start.2
  82.6 2.7 %fusion = (bf16[4,6,24,512]{3,2,1,0:T(8,128)(2,1)}, bf16[4,6,24,512]{3,2,1,0:T(8,128)(2,1)}) fusion(bf16[4,6,24,512]{3,2,1,0:T(8,128)(2,1)} %bitcast.28, bf16[4,6,24,512]{3,2,1,0:T(8,128)(2,1)S(1)} %copy-done.1, bf16[4,6,24,512]{3,2,1,0:T(8,128)(2,1)} %bitcast.27, bf16[4,6,24,512]{3,2,1,0:T(8,128)(2,1)S(1)} %copy-done), kind=kLoop, calls=%fused_computation.2 | loop fusion | flops 2359296 | bytes 3538944 | tf_op jit(solution)/shard_map/convert_element_type | solution.py:432
  85.3 0.0 copy-done.2
  85.4 0.1 slice.8
  85.5 0.5 copy.13
  86.0 1.0 %copy.14 = f32[64,8,2,256]{3,1,2,0:T(8,128)} copy(f32[64,8,2,256]{3,2,1,0:T(2,128)S(1)} %bitcast.20) | data formatting | bytes 2097152
  87.1 1.6 %copy.16 = f32[2,3,512,256]{3,0,1,2:T(2,128)S(1)} copy(bf16[2,3,512,256]{3,2,1,0:T(8,128)(2,1)S(1)} %bitcast.19) | data formatting | bytes 4718592 | tf_op jit(solution)/shard_map/convert_element_type | solution.py:436
  88.7 3.7 %reshape.40 = f32[512,1536]{1,0:T(8,128)} reshape(f32[512,3,2,256]{3,2,1,0:T(2,128)S(1)} %bitcast.18) | data formatting | bytes 6291456 | tf_op jit(solution)/shard_map/convert_element_type | solution.py:436
  (1 shorter events, 0.0 us)
Async XLA Ops:
  0.6 81.9 %copy-start = (bf16[4,6,24,512]{3,2,1,0:T(8,128)(2,1)S(1)}, bf16[4,6,24,512]{3,2,1,0:T(8,128)(2,1)}, u32[]{:S(2)}) copy-start(bf16[4,6,24,512]{3,2,1,0:T(8,128)(2,1)} %param.8) | copy-start | bytes 1769476
  0.6 81.9 %copy-start.1 = (bf16[4,6,24,512]{3,2,1,0:T(8,128)(2,1)S(1)}, bf16[4,6,24,512]{3,2,1,0:T(8,128)(2,1)}, u32[]{:S(2)}) copy-start(bf16[4,6,24,512]{3,2,1,0:T(8,128)(2,1)} %param.9) | copy-start | bytes 1769476
  82.6 2.8 %copy-start.2 = (bf16[2,2,64,16,256]{4,3,2,1,0:T(8,128)(2,1)S(1)}, bf16[2,2,64,16,256]{4,3,2,1,0:T(8,128)(2,1)}, u32[]{:S(2)}) copy-start(bf16[2,2,64,16,256]{4,3,2,1,0:T(8,128)(2,1)} %get-tuple-element.9) | copy-start | bytes 6291460

commit v3 on v2

--- a/solution.py
+++ b/solution.py
@@ -145,23 +145,46 @@
 
 
 def weight_gradients(g, normed, cot, ctx, dqkv, grad):
+    def keep(d, half, at, count):
+        for b in range(2):
+            piece = d[:, 128 * b : 128 * b + 128].astype(BF)
+            grad[g, half, b, at : at + count] = piece.reshape(count, 16, 128)
+
     for part in range(3):
-        d = dot(normed[...], dqkv[g, :, 256 * part : 256 * part + 256], TN).astype(BF)
-        at = 32 * (part % 2)
-        grad[g, part // 2, at : at + 32] = d.reshape(32, 16, 256)
+        d = dot(normed[...], dqkv[g, :, 256 * part : 256 * part + 256], TN)
+        keep(d, part // 2, 32 * (part % 2), 32)
     for half in range(2):
-        d = dot(ctx[g], cot[:, 256 * half : 256 * half + 256], TN).astype(BF)
-        at = 32 + 16 * half
-        grad[g, 1, at : at + 16] = d.reshape(16, 16, 256)
+        d = dot(ctx[g], cot[:, 256 * half : 256 * half + 256], TN)
+        keep(d, 1, 32 + 16 * half, 16)
 
 
 def place():
     lat, lon = lax.axis_index("lat"), lax.axis_index("lon")
-    return lat * 8 + lon // 2, lon % 2
-
-
-def device(chip, core):
-    return chip // 8, (chip % 8) * 2 + core
+    return (lon // 2) % 4, (lon // 8) * 2 + lat % 2, lat // 2, lon % 2
+
+
+def device(x, y, z, core):
+    return z * 2 + y % 2, ((y // 2) * 4 + x) * 2 + core
+
+
+def first_at(b):
+    x, y, z, core = place()
+    return x if b == 0 else z
+
+
+def first_device(b, to):
+    x, y, z, core = place()
+    return device(to, y, z, core) if b == 0 else device(x, y, to, core)
+
+
+def second_at(b):
+    x, y, z, core = place()
+    return y * 4 + (z if b == 0 else x)
+
+
+def second_device(b, to):
+    x, y, z, core = place()
+    return device(x, to // 4, to % 4, core) if b == 0 else device(to % 4, to // 4, z, core)
 
 
 def beside(lat_step, lon_step):
@@ -174,19 +197,26 @@
 
 
 def greet():
-    chip, core = place()
+    x, y, z, core = place()
     barrier = pltpu.get_barrier_semaphore()
-    for steps in ((0, -1), (0, 1), (-1, -1), (1, 1)):
-        pl.semaphore_signal(barrier, inc=1, device_id=beside(*steps), device_id_type=MESH)
-    pl.semaphore_signal(barrier, inc=1, device_id=device(chip, 1 - core), device_id_type=MESH)
-
-    @pl.loop(1, 64)
-    def _(t):
-        pl.semaphore_signal(barrier, inc=1, device_id=device(chip ^ t, core), device_id_type=MESH)
+
+    def signal(to):
+        pl.semaphore_signal(barrier, inc=1, device_id=to, device_id_type=MESH)
+
+    for steps in ((-1, 0), (0, -1), (-1, -1), (1, 0), (0, 1), (1, 1)):
+        signal(beside(*steps))
+    signal(device(x, y, z, 1 - core))
+    for b in range(2):
+        for k in range(1, 4):
+            signal(first_device(b, first_at(b) ^ k))
+
+        @pl.loop(1, 16)
+        def _(t):
+            signal(second_device(b, second_at(b) ^ t))
 
 
 def meet():
-    pl.semaphore_wait(pltpu.get_barrier_semaphore(), 68)
+    pl.semaphore_wait(pltpu.get_barrier_semaphore(), 43)
 
 
 def halo(p, step, src, dst, send, recv):
@@ -202,43 +232,70 @@
 
 
 def core_swap(src, dst, send, recv):
-    chip, core = place()
+    x, y, z, core = place()
     return pltpu.make_async_remote_copy(
         src_ref=src, dst_ref=dst, send_sem=send, recv_sem=recv,
-        device_id=device(chip, 1 - core), device_id_type=MESH,
+        device_id=device(x, y, z, 1 - core), device_id_type=MESH,
     )
 
 
-def scatter_start(mixed, parts, send, recv):
-    chip, core = place()
-
-    @pl.loop(1, 64)
-    def _(t):
-        pltpu.make_async_remote_copy(
-            src_ref=mixed.at[chip ^ t], dst_ref=parts.at[chip], send_sem=send, recv_sem=recv,
-            device_id=device(chip ^ t, core), device_id_type=MESH,
-        ).start()
-
-
-def gather_start(total, send, recv):
-    chip, core = place()
-
-    @pl.loop(1, 64)
-    def _(t):
-        pltpu.make_async_remote_copy(
-            src_ref=total.at[core, chip], dst_ref=total.at[core, chip], send_sem=send, recv_sem=recv,
-            device_id=device(chip ^ t, core), device_id_type=MESH,
-        ).start()
+def scatter_first(mixed, parts, send, recv):
+    for b in range(2):
+        at = first_at(b)
+        for k in (2, 1, 3):
+            pltpu.make_async_remote_copy(
+                src_ref=mixed.at[b, pl.ds((at ^ k) * 16, 16)], dst_ref=parts.at[b, at],
+                send_sem=send.at[b], recv_sem=recv.at[b],
+                device_id=first_device(b, at ^ k), device_id_type=MESH,
+            ).start()
+
+
+def scatter_second(mixed, parts, send, recv):
+    for b in range(2):
+        at = second_at(b)
+
+        @pl.loop(0, 15)
+        def _(t):
+            to = at ^ (15 - t)
+            pltpu.make_async_remote_copy(
+                src_ref=mixed.at[b, to], dst_ref=parts.at[b, at],
+                send_sem=send.at[b], recv_sem=recv.at[b],
+                device_id=second_device(b, to), device_id_type=MESH,
+            ).start()
+
+
+def gather_second(total, send, recv):
+    for b in range(2):
+        at = second_at(b)
+        piece = total.at[b, first_at(b) * 16 + at]
+
+        @pl.loop(0, 15)
+        def _(t):
+            pltpu.make_async_remote_copy(
+                src_ref=piece, dst_ref=piece, send_sem=send.at[b], recv_sem=recv.at[b],
+                device_id=second_device(b, at ^ (15 - t)), device_id_type=MESH,
+            ).start()
+
+
+def gather_first(total, send, recv):
+    for b in range(2):
+        at = first_at(b)
+        piece = total.at[b, pl.ds(at * 16, 16)]
+        for k in (2, 1, 3):
+            pltpu.make_async_remote_copy(
+                src_ref=piece, dst_ref=piece, send_sem=send.at[b], recv_sem=recv.at[b],
+                device_id=first_device(b, at ^ k), device_id_type=MESH,
+            ).start()
 
 
 def kernel(
     tokens, cotangent, w_qkv_in, w_proj_in, pack_in, place_in, unplace_in, unpack_in,
-    att, dflat, total,
+    output, grad_tokens, gqkv, gproj,
     both, w_qkv, w_proj, pack, place_m, unplace, unpack, out_halo, in_halo, out_back, in_back,
     tok, cot, hat, normed, inv, q, k, v, dc, qs, cs, pt, st, sf, df, ctx, dqkv, done,
-    grad, swapped, mixed, parts, load, send, recv, hsend, hrecv, bsend, brecv,
+    grad, swapped, mixed, parts, mixed2, parts2, total, load, swap_send, swap_recv, send, recv, hsend, hrecv, bsend, brecv,
 ):
-    chip, core = place()
+    x, y, z, core = place()
     greet()
     loads = []
 
@@ -293,13 +350,73 @@
         attend(g, w, lat_last, lon_last, mask, maskf, q, k, v, dc, qs, cs, pt, st, sf, df, ctx, dqkv)
 
     def swap_in(g):
-        return core_swap(grad.at[g, 1 - core], swapped.at[g], send.at[g, 0], recv.at[g, 0])
-
-    def mix(g):
+        return core_swap(grad.at[g, 1 - core], swapped.at[g], swap_send.at[g, 0], swap_recv.at[g, 0])
+
+    def swap_out(g):
+        part = total.at[g, core]
+        return core_swap(part, part, swap_send.at[g, 1], swap_recv.at[g, 1])
+
+    def sum_first(g):
         swap_in(g).wait()
         mixed[g] = (grad[g, core].astype(F32) + swapped[g].astype(F32)).astype(BF)
-        scatter_start(mixed.at[g], parts.at[g], send.at[g, 1], recv.at[g, 1])
-        parts[g, chip] = mixed[g, chip]
+        scatter_first(mixed.at[g], parts.at[g], send.at[g, 0], recv.at[g, 0])
+        for b in range(2):
+            at = first_at(b)
+            parts[g, b, at] = mixed[g, b, pl.ds(at * 16, 16)]
+
+    def sum_second(g):
+        for b in range(2):
+            drain(parts.at[g, b, pl.ds(0, 3)], recv.at[g, 0, b])
+            mixed2[g, b] = jnp.sum(parts[g, b].astype(F32), axis=0).astype(BF)
+        scatter_second(mixed2.at[g], parts2.at[g], send.at[g, 1], recv.at[g, 1])
+        for b in range(2):
+            at = second_at(b)
+            parts2[g, b, at] = mixed2[g, b, at]
+
+    def spread_second(g):
+        for b in range(2):
+            drain(parts2.at[g, b, pl.ds(0, 15)], recv.at[g, 1, b])
+            final = jnp.sum(parts2[g, b].astype(F32), axis=0) * NORM
+            total[g, core, b, first_at(b) * 16 + second_at(b)] = final.astype(BF)
+        gather_second(total.at[g, core], send.at[g, 2], recv.at[g, 2])
+
+    def spread_first(g):
+        for b in range(2):
+            drain(parts2.at[g, b, pl.ds(0, 15)], recv.at[g, 2, b])
+        gather_first(total.at[g, core], send.at[g, 3], recv.at[g, 3])
+
+    def spread_core(g):
+        for b in range(2):
+            drain(parts.at[g, b, pl.ds(0, 3)], recv.at[g, 3, b])
+        swap_out(g).start()
+
+    def drain_sends(g):
+        for b in range(2):
+            for i, ref in enumerate((parts, parts2, parts2, parts)):
+                drain(ref.at[g, b, pl.ds(0, 15 if i in (1, 2) else 3)], send.at[g, i, b])
+
+    def write_gradients(g):
+        swap_out(g).wait()
+        for b in range(2):
+            for part in range(3):
+                at = 512 * part + 256 * g + 128 * b
+                rows = slice(32 * (part % 2), 32 * (part % 2) + 32)
+                gqkv[:, at : at + 128] = total[g, part // 2, b, rows].reshape(512, 128)
+            for half in range(2):
+                at = 256 * half + 128 * b
+                rows = slice(32 + 16 * half, 48 + 16 * half)
+                gproj[256 * g : 256 * g + 256, at : at + 128] = total[g, 1, b, rows].reshape(256, 128)
+
+    def back(p):
+        in_back[p, 0:224] = out_back[p, 0:224]
+        for copy in going[p]:
+            copy.wait_recv()
+        for half, out in enumerate((output, grad_tokens)):
+            for level in range(2):
+                at = 144 * ((2 * p + 1 + level) % 4)
+                rows = slice(288 * half + 144 * level, 288 * half + 144 * level + 144)
+                moved = dot(unpack[rows, :], in_back[p])
+                out[at : at + 144, :] = (both[p, rows, :].astype(F32) + moved).astype(BF)
 
     def leave(p):
         @pl.loop(0, 2)
@@ -317,6 +434,7 @@
     def _(i):
         attention(i // 2, i % 2)
 
+    leave(0)
     arrive(1)
 
     @pl.loop(0, 2)
@@ -325,42 +443,32 @@
         def _(w):
             attention(g, w)
 
+        @pl.when(g == 1)
+        def _():
+            sum_first(0)
+
         weight_gradients(g, normed, cot, ctx, dqkv, grad)
         swap_in(g).start()
 
-        @pl.when(g == 1)
-        def _():
-            mix(0)
-
-    leave(0)
-    mix(1)
     leave(1)
-    for g in range(2):
-        drain(parts.at[g, pl.ds(0, 63)], recv.at[g, 1])
-        acc = jnp.sum(parts[g].astype(F32), axis=0) * NORM
-        total[g, core, chip] = acc.astype(BF)
-        gather_start(total.at[g], send.at[g, 2], recv.at[g, 2])
-    for p in range(2):
-        in_back[p, 0:224] = out_back[p, 0:224]
-        for copy in going[p]:
-            copy.wait_recv()
-        for half, out in enumerate((att, dflat)):
-            for level in range(2):
-                at = 144 * ((2 * p + 1 + level) % 4)
-                rows = slice(288 * half + 144 * level, 288 * half + 144 * level + 144)
-                out[at : at + 144, :] = dot(unpack[rows, :], in_back[p]).astype(BF)
-    swaps = []
-    for g in range(2):
-        drain(parts.at[g, pl.ds(0, 63)], recv.at[g, 2])
-        swaps.append(core_swap(total.at[g, core], total.at[g, core], send.at[g, 3], recv.at[g, 3]))
-        swaps[g].start()
-    for g in range(2):
-        swaps[g].wait()
-        for i in range(1, 3):
-            drain(parts.at[g, pl.ds(0, 63)], send.at[g, i])
+    sum_first(1)
+    sum_second(0)
+    back(0)
+    sum_second(1)
+    spread_second(0)
+    spread_second(1)
+    spread_first(0)
+    back(1)
+    spread_first(1)
+    spread_core(0)
+    drain_sends(0)
     for p in range(2):
         for copy in coming[p] + going[p]:
             copy.wait_send()
+    write_gradients(0)
+    spread_core(1)
+    drain_sends(1)
+    write_gradients(1)
 
 
 def block(tokens, cotangent, w_qkv, w_proj):
@@ -372,10 +480,11 @@
         out_shape=(
             jax.ShapeDtypeStruct((576, 512), BF),
             jax.ShapeDtypeStruct((576, 512), BF),
-            jax.ShapeDtypeStruct((2, 2, 64, 16, 256), BF),
+            jax.ShapeDtypeStruct((512, 1536), BF),
+            jax.ShapeDtypeStruct((512, 512), BF),
         ),
         in_specs=[hbm] * 8,
-        out_specs=(vm,) * 3,
+        out_specs=(vm,) * 4,
         scratch_shapes=[
             pltpu.VMEM((2, 576, 512), BF),
             pltpu.VMEM((512, 1536), BF),
@@ -406,13 +515,18 @@
             pltpu.VMEM((2, 576, 256), BF),
             pltpu.VMEM((2, 576, 768), BF),
             pltpu.VMEM((2, 576, 512), BF),
-            pltpu.VMEM((2, 2, 64, 16, 256), BF),
-            pltpu.VMEM((2, 64, 16, 256), BF),
-            pltpu.VMEM((2, 64, 16, 256), BF),
-            pltpu.VMEM((2, 64, 16, 256), BF),
+            pltpu.VMEM((2, 2, 2, 64, 16, 128), BF),
+            pltpu.VMEM((2, 2, 64, 16, 128), BF),
+            pltpu.VMEM((2, 2, 64, 16, 128), BF),
+            pltpu.VMEM((2, 2, 4, 16, 16, 128), BF),
+            pltpu.VMEM((2, 2, 16, 16, 128), BF),
+            pltpu.VMEM((2, 2, 16, 16, 128), BF),
+            pltpu.VMEM((2, 2, 2, 64, 16, 128), BF),
             dma((16,)),
-            dma((2, 4)),
-            dma((2, 4)),
+            dma((2, 2)),
+            dma((2, 2)),
+            dma((2, 4, 2)),
+            dma((2, 4, 2)),
             dma((2, 3)),
             dma((2, 3)),
             dma((2, 3)),
@@ -427,13 +541,10 @@
 
 def body(tokens, cotangent, w_qkv, w_proj):
     shape = tokens.shape
-    att, dflat, total = block(tokens.reshape(576, 512), cotangent.reshape(576, 512), w_qkv, w_proj)
-    output = (tokens.astype(F32) + att.reshape(shape).astype(F32)).astype(BF)
-    grad_tokens = (cotangent.astype(F32) + dflat.reshape(shape).astype(F32)).astype(BF)
-    total = total.reshape(2, 2048, 256)
-    gqkv = total[:, :1536].reshape(2, 3, 512, 256).transpose(2, 1, 0, 3).reshape(512, 1536)
-    gproj = total[:, 1536:].reshape(2, 2, 256, 256).transpose(0, 2, 1, 3).reshape(512, 512)
-    return (output, grad_tokens, gqkv.astype(F32), gproj.astype(F32))
+    output, grad_tokens, gqkv, gproj = block(
+        tokens.reshape(576, 512), cotangent.reshape(576, 512), w_qkv, w_proj
+    )
+    return (output.reshape(shape), grad_tokens.reshape(shape), gqkv.astype(F32), gproj.astype(F32))
 
 
 def solution(mesh):

time: 92.5 us -> 79 us (0.85)
  Pallas kernels: 81.9 us -> 71.9 us
  local copies, waits for them, and re-layouts: 7.04 us -> 1.67 us
  other arithmetic: 2.74 us -> 4.64 us
    pallas_call x1, Pallas kernels: 81.9 us -> 71.9 us  [block(): pl.pallas_call(kernel, out_shape=(jax.ShapeDtypeStruct((576, 512), BF), j...]
    convert_element_type x3 -> x0, local copies, waits for them, and re-layouts: 5.85 us -> none  [body(): return (output, grad_tokens, gqkv.astype(F32), gproj.astype(F32))]
    convert_element_type x1 -> x2, other arithmetic: 2.74 us -> 4.64 us  [the longest x1 3.54 us: body(): gqkv.astype(F32)]
where the time goes in v3:
time: 79 us; the launch traced here: 78.8 us
  Pallas kernels  71.9 us (91%)
  other arithmetic  4.64 us (6%)
  local copies, waits for them, and re-layouts  1.67 us (2%)
    pallas_call x1, Pallas kernels, block(): pl.pallas_call(kernel, out_shape=(jax.ShapeDtypeStruct((576, 512), BF), j...  71.9 us
    convert_element_type x1, other arithmetic, body(): gqkv.astype(F32)  3.54 us
    unnamed x8, local copies, waits for them, and re-layouts  1.67 us

profile of v3, /device:TPU:1, one launch (start us, length us, event | category | flops | bytes accessed | tf_op | source)
XLA Modules:
  0.0 78.8 jit_solution(2819681507625415668)
XLA Ops:
  0.6 71.9 %window_block.1 = (bf16[576,512]{1,0:T(8,128)(2,1)}, bf16[576,512]{1,0:T(8,128)(2,1)}, bf16[512,1536]{1,0:T(8,128)(2,1)}, bf16[512,512]{1,0:T(8,128)(2,1)}) custom-call(bf16[576,512]{1,0:T(8,128)(2,1)} %bitcast.4, bf16[576,512]{1,0:T(8,128)(2,1)} %bitcast.5, bf16[512,1536]{1,0:T(8,128)(2,1)} %w_qkv_in.1, bf16[512,512]{1,0:T(8,128)(2,1)} %w_proj_in.1, ...), custom_call_target="tpu_custom_call" | custom-call | tf_op jit(solution)/shard_map/window_block/pallas_call | solution.py:478
  72.5 0.0 copy-start.2
  72.5 3.5 %convert_element_type.6 = f32[512,1536]{1,0:T(8,128)} convert(bf16[512,1536]{1,0:T(8,128)(2,1)} %get-tuple-element.10) | non-fusion elementwise | flops 786432 | bytes 4718592 | tf_op jit(solution)/shard_map/convert_element_type | solution.py:547
  76.1 0.0 copy-start.1
  76.1 0.0 copy-start
  76.1 0.0 copy-done.2
  76.1 1.1 %convert_element_type.7 = f32[512,512]{1,0:T(8,128)} convert(bf16[512,512]{1,0:T(8,128)(2,1)S(1)} %copy-done.2) | non-fusion elementwise | flops 262144 | bytes 1572864 | tf_op jit(solution)/shard_map/convert_element_type | solution.py:547
  77.2 0.0 copy-done.1
  77.2 0.8 %copy.14 = bf16[4,6,24,512]{3,2,1,0:T(8,128)(2,1)} copy(bf16[4,6,24,512]{3,2,1,0:T(8,128)(2,1)S(1)} %bitcast.7) | data formatting | bytes 1179648
  78.0 0.0 copy-done
  78.0 0.8 %copy.15 = bf16[4,6,24,512]{3,2,1,0:T(8,128)(2,1)} copy(bf16[4,6,24,512]{3,2,1,0:T(8,128)(2,1)S(1)} %bitcast.6) | data formatting | bytes 1179648
Async XLA Ops:
  72.5 3.6 %copy-start.2 = (bf16[512,512]{1,0:T(8,128)(2,1)S(1)}, bf16[512,512]{1,0:T(8,128)(2,1)}, u32[]{:S(2)}) copy-start(bf16[512,512]{1,0:T(8,128)(2,1)} %get-tuple-element.11) | copy-start | bytes 1572868
  76.1 1.1 %copy-start.1 = (bf16[576,512]{1,0:T(8,128)(2,1)S(1)}, bf16[576,512]{1,0:T(8,128)(2,1)}, u32[]{:S(2)}) copy-start(bf16[576,512]{1,0:T(8,128)(2,1)} %get-tuple-element.8) | copy-start | bytes 1769476
  76.1 2.0 %copy-start = (bf16[576,512]{1,0:T(8,128)(2,1)S(1)}, bf16[576,512]{1,0:T(8,128)(2,1)}, u32[]{:S(2)}) copy-start(bf16[576,512]{1,0:T(8,128)(2,1)} %get-tuple-element.9) | copy-start | bytes 1769476

commit v4 on v3

v4 whole, which is shorter than its diff:
```python
import numpy as np
import jax
import jax.numpy as jnp
from jax import lax
from jax.experimental import pallas as pl
from jax.experimental.pallas import tpu as pltpu
from jax.sharding import PartitionSpec as P

BF = jnp.bfloat16
F32 = jnp.float32
SCALE = 1.0 / 32**0.5
EXP2 = SCALE * 1.4426950408889634
NORM = 1.0 / 73728**0.5
NN = (((1,), (0,)), ((), ()))
NT = (((1,), (1,)), ((), ()))
TN = (((0,), (0,)), ((), ()))
MESH = pl.DeviceIdType.MESH

STARTS = (0, 224, 448, 528)
ROWS = 608
SECTIONS = ((224, 224), (448, 80), (528, 80))


def section_row(array, level, row, col):
    section = (2 if col < 6 else 0) + (1 if row < 3 else 0)
    width, first = (18, 6) if col >= 6 else (6, 0)
    at = (level * 3 + row % 3) * width + col - first
    return STARTS[section] + array * 6 * width + at


def orders():
    pack = np.zeros((ROWS, 576), np.float32)
    place = np.zeros((576, ROWS), np.float32)
    for array in range(2):
        for level in range(2):
            for row in range(6):
                for col in range(24):
                    at = array * 288 + level * 144 + row * 24 + col
                    pack[section_row(array, level, row, col), at] = 1
            for row in range(6):
                for col in range(24):
                    at = array * 288 + col // 12 * 144 + level * 72 + row * 12 + col % 12
                    source = section_row(array, level, (row + 3) % 6, (col + 6) % 24)
                    place[at, source] = 1
    return [jnp.asarray(m, BF) for m in (pack, place, place.T, pack.T)]


def dot(a, b, dims=NN):
    return lax.dot_general(a, b, dims, preferred_element_type=F32)


def head_mask(dtype):
    head = lax.broadcasted_iota(jnp.int32, (128, 256), 0) >> 4
    col = lax.broadcasted_iota(jnp.int32, (128, 256), 1) >> 5
    return (head == col).astype(dtype)


def window_rows(w):
    return pl.ds(pl.multiple_of(w * 144, 16), 144)


def pair_rows(p):
    return slice(288 * p, 288 * p + 288)


def project(p, tok, cot, w_qkv, w_proj_t, hat, normed, inv, q, k, v, dc):
    rows = pair_rows(p)
    x = tok[rows, :].astype(F32)
    x = x - jnp.mean(x, axis=1, keepdims=True)
    scale = lax.rsqrt(jnp.mean(x * x, axis=1, keepdims=True) + 1e-05)
    x = x * scale
    hat[rows, :] = x
    inv[rows, :] = jnp.broadcast_to(scale, (288, 128))
    x = x.astype(BF)
    normed[rows, :] = x
    for g in range(2):
        for part, ref in enumerate((q, k, v)):
            at = 512 * part + 256 * g
            ref[g, rows, :] = dot(x, w_qkv[:, at : at + 256]).astype(BF)
        dc[g, rows, :] = dot(cot[rows, :], w_proj_t[:, 256 * g : 256 * g + 256]).astype(BF)


def key_rows(p, c):
    if p == 0 or c == 4:
        return slice(0, 144)
    return slice(0, 80) if c < 4 else slice(64, 144)


def spans(p):
    if p == 0:
        return [(slice(0, 144), slice(0, 1152))]
    return [(key_rows(p, c), slice(128 * c, 128 * d)) for c, d in ((0, 4), (4, 5), (5, 9))]


def attend(p, g, lat_last, lon_last, mask, maskf, q, k, v, dc, qs, cs, pt, st, sf, df, ctx, dqkv):
    def rows(i):
        return slice(144 * (2 * p + i), 144 * (2 * p + i) + 144)

    def scores(i):
        first = 144 * (2 * p + i)
        keys, vals = k[g, rows(i), :], v[g, rows(i), :]
        for c in range(9):
            at = slice(128 * c, 128 * c + 128)
            q16 = q[g, first + 16 * c : first + 16 * c + 16, :]
            d16 = dc[g, first + 16 * c : first + 16 * c + 16, :]
            qs[i, at, :] = jnp.concatenate([q16] * 8, axis=0) * mask
            cs[i, at, :] = jnp.concatenate([d16] * 8, axis=0) * mask
        for kr, at in spans(p):
            sf[i, kr, at] = dot(keys[kr], qs[i, at, :], NT)
            df[i, kr, at] = dot(vals[kr], cs[i, at, :], NT)

    def softmax(i):
        klab, qlab = labels(2 * p + i, lat_last, lon_last)
        for c in range(9):
            at = slice(128 * c, 128 * c + 128)
            kr = key_rows(p, c)
            s = jnp.where(klab[kr] == qlab[c], sf[i, kr, at], -1e30)
            e = jnp.exp2((s - jnp.max(s, axis=0, keepdims=True)) * EXP2)
            prob = e * (1.0 / jnp.sum(e, axis=0, keepdims=True))
            pt[2 * p + i, kr, at] = prob.astype(BF)
            dp = df[i, kr, at]
            inner = jnp.sum(prob * dp, axis=0, keepdims=True)
            st[2 * p + i, kr, at] = ((prob * SCALE) * (dp - inner)).astype(BF)

    def fold(m, i, ref):
        out = [dot(m[2 * p + i, kr, at], ref[g, rows(i), :][kr], TN) for kr, at in spans(p)]
        out = jnp.concatenate(out, axis=0) if len(out) > 1 else out[0]
        out = out.reshape(9, 8, 16, 256) * maskf.reshape(1, 8, 16, 256)
        return jnp.sum(out, axis=1).reshape(144, 256).astype(BF)

    def columns(part):
        return pl.ds(pl.multiple_of(768 * g + 256 * part, 256), 256)

    def results(i):
        ctx[rows(i), pl.ds(pl.multiple_of(256 * g, 256), 256)] = fold(pt, i, v)
        dqkv[rows(i), columns(0)] = fold(st, i, k)
        dqkv[rows(i), columns(1)] = dot(st[2 * p + i], qs[i]).astype(BF)
        dqkv[rows(i), columns(2)] = dot(pt[2 * p + i], cs[i]).astype(BF)

    scores(0)
    scores(1)
    softmax(0)
    results(0)
    softmax(1)
    results(1)


def finish(p, w_qkv_t, w_proj, hat, inv, ctx, dqkv, done):
    rows = pair_rows(p)
    done[p, 0:288, :] = dot(ctx[rows, :], w_proj[...]).astype(BF)
    d = dot(dqkv[rows, :], w_qkv_t[...])
    h = hat[rows, :]
    d = d - jnp.mean(d, axis=1, keepdims=True) - h * jnp.mean(d * h, axis=1, keepdims=True)
    scale = jnp.concatenate([inv[rows, :]] * 4, axis=1)
    done[p, 288:576, :] = (d * scale).astype(BF)


def labels(w, lat_last, lon_last):
    def flags(t):
        level = (t >= 72).astype(jnp.int32)
        t = t - 72 * level
        row = (t >= 36).astype(jnp.int32)
        t = t - 36 * row
        t = jnp.where(t >= 24, t - 24, jnp.where(t >= 12, t - 12, t))
        col = (t >= 6).astype(jnp.int32)
        return level * is_b + row * lat_last + col * last

    is_b = 4 * (w // 2)
    last = lon_last * (w % 2)
    klab = flags(lax.broadcasted_iota(jnp.int32, (144, 128), 0))
    lane = lax.broadcasted_iota(jnp.int32, (1, 128), 1) & 15
    qlab = [flags(lane + 16 * c) for c in range(9)]
    return klab, qlab


def weight_gradients(g, normed, cot, ctx, dqkv, grad):
    def keep(d, half, at, count):
        for b in range(2):
            piece = d[:, 128 * b : 128 * b + 128].astype(BF)
            grad[g, half, b, at : at + count] = piece.reshape(count, 16, 128)

    for part in range(3):
        at = 768 * g + 256 * part
        d = dot(normed[...], dqkv[:, at : at + 256], TN)
        keep(d, part // 2, 32 * (part % 2), 32)
    d = dot(ctx[:, 256 * g : 256 * g + 256], cot[...], TN)
    for half in range(2):
        keep(d[:, 256 * half : 256 * half + 256], 1, 32 + 16 * half, 16)


def place():
    lat, lon = lax.axis_index("lat"), lax.axis_index("lon")
    return (lon // 2) % 4, (lon // 8) * 2 + lat % 2, lat // 2, lon % 2


def device(x, y, z, core):
    return z * 2 + y % 2, ((y // 2) * 4 + x) * 2 + core


def first_at(b):
    x, y, z, core = place()
    return x if b == 0 else z


def first_device(b, to):
    x, y, z, core = place()
    return device(to, y, z, core) if b == 0 else device(x, y, to, core)


def second_at(b):
    x, y, z, core = place()
    return y * 4 + (z if b == 0 else x)


def second_device(b, to):
    x, y, z, core = place()
    return device(x, to // 4, to % 4, core) if b == 0 else device(to % 4, to // 4, z, core)


def beside(lat_step, lon_step):
    lat, lon = lax.axis_index("lat"), lax.axis_index("lon")
    return lax.rem(lat + lat_step + 8, 8), lax.rem(lon + lon_step + 16, 16)


def drain(ref, sem):
    pltpu.make_async_copy(ref, ref, sem).wait()


def greet():
    x, y, z, core = place()
    barrier = pltpu.get_barrier_semaphore()

    def signal(to):
        pl.semaphore_signal(barrier, inc=1, device_id=to, device_id_type=MESH)

    for steps in ((-1, 0), (0, -1), (-1, -1), (1, 0), (0, 1), (1, 1)):
        signal(beside(*steps))
    signal(device(x, y, z, 1 - core))
    for b in range(2):
        for k in range(1, 4):
            signal(first_device(b, first_at(b) ^ k))

        @pl.loop(1, 16)
        def _(t):
            signal(second_device(b, second_at(b) ^ t))


def meet():
    pl.semaphore_wait(pltpu.get_barrier_semaphore(), 43)


def halo(p, step, src, dst, send, recv):
    copies = []
    for s, (at, count) in enumerate(SECTIONS):
        lat_step, lon_step = ((step, 0), (0, step), (step, step))[s]
        copies.append(pltpu.make_async_remote_copy(
            src_ref=src.at[p, pl.ds(at, count)], dst_ref=dst.at[p, pl.ds(at, count)],
            send_sem=send.at[p, s], recv_sem=recv.at[p, s],
            device_id=beside(lat_step, lon_step), device_id_type=MESH,
        ))
    return copies


def core_swap(src, dst, send, recv):
    x, y, z, core = place()
    return pltpu.make_async_remote_copy(
        src_ref=src, dst_ref=dst, send_sem=send, recv_sem=recv,
        device_id=device(x, y, z, 1 - core), device_id_type=MESH,
    )


def scatter_first(mixed, parts, send, recv):
    for b in range(2):
        at = first_at(b)
        for k in (2, 1, 3):
            pltpu.make_async_remote_copy(
                src_ref=mixed.at[b, pl.ds((at ^ k) * 16, 16)], dst_ref=parts.at[b, at],
                send_sem=send.at[b], recv_sem=recv.at[b],
                device_id=first_device(b, at ^ k), device_id_type=MESH,
            ).start()


def scatter_second(mixed, parts, send, recv):
    for b in range(2):
        at = second_at(b)

        @pl.loop(0, 15)
        def _(t):
            to = at ^ (15 - t)
            pltpu.make_async_remote_copy(
                src_ref=mixed.at[b, to], dst_ref=parts.at[b, at],
                send_sem=send.at[b], recv_sem=recv.at[b],
                device_id=second_device(b, to), device_id_type=MESH,
            ).start()


def gather_second(total, send, recv):
    for b in range(2):
        at = second_at(b)
        piece = total.at[b, first_at(b) * 16 + at]

        @pl.loop(0, 15)
        def _(t):
            pltpu.make_async_remote_copy(
                src_ref=piece, dst_ref=piece, send_sem=send.at[b], recv_sem=recv.at[b],
                device_id=second_device(b, at ^ (15 - t)), device_id_type=MESH,
            ).start()


def gather_first(b, total, send, recv):
    at = first_at(b)
    piece = total.at[b, pl.ds(at * 16, 16)]
    for k in (2, 1, 3):
        pltpu.make_async_remote_copy(
            src_ref=piece, dst_ref=piece, send_sem=send.at[b, k], recv_sem=recv.at[b, k],
            device_id=first_device(b, at ^ k), device_id_type=MESH,
        ).start()


def kernel(
    tokens, cotangent, w_qkv_in, w_proj_in, pack_in, place_in, unplace_in, unpack_in,
    output, grad_tokens, gqkv_out, gproj_out,
    moved, gqkv, gproj, both, w_qkv, w_proj, w_qkv_t, w_proj_t, pack, place_m, unplace, unpack, out_halo, in_halo, out_back, in_back,
    tok, cot, hat, normed, inv, q, k, v, dc, qs, cs, pt, st, sf, df, ctx, dqkv, done,
    grad, swapped, mixed, parts, mixed2, parts2, total, load, store, swap_send, swap_recv, send, recv, core_send, core_recv, wide_send, wide_recv, hsend, hrecv, bsend, brecv,
):
    x, y, z, core = place()
    greet()
    loads = []

    def fetch(src, dst):
        copy = pltpu.make_async_copy(src, dst, load.at[len(loads)])
        copy.start()
        loads.append(copy)

    for p in range(2):
        for half, src in enumerate((tokens, cotangent)):
            for level in range(2):
                fetch(
                    src.at[pl.ds(144 * ((2 * p + 1 + level) % 4), 144)],
                    both.at[p, pl.ds(288 * half + 144 * level, 144)],
                )
    fetch(pack_in, pack)
    early = len(loads)
    fetch(place_in, place_m)
    fetch(w_qkv_in, w_qkv)
    fetch(w_proj_in, w_proj)
    fetch(unplace_in, unplace)
    fetch(unpack_in, unpack)
    for copy in loads[:early]:
        copy.wait()
    out_halo[0] = dot(pack[...], both[0]).astype(BF)
    meet()
    coming = [halo(p, -1, out_halo, in_halo, hsend, hrecv) for p in range(2)]
    for copy in coming[0]:
        copy.start()
    out_halo[1] = dot(pack[...], both[1]).astype(BF)
    for copy in coming[1]:
        copy.start()
    for copy in loads[early:]:
        copy.wait()
    for g in range(2):
        for part in range(3):
            at = 512 * part + 256 * g
            to = 768 * g + 256 * part
            w_qkv_t[to : to + 256, :] = w_qkv[:, at : at + 256].T
    w_proj_t[...] = w_proj[...].T
    for i in range(2):
        pt[2 + i] = jnp.zeros((144, 1152), BF)
        st[2 + i] = jnp.zeros((144, 1152), BF)
    lat_last = 2 * (lax.axis_index("lat") == 7).astype(jnp.int32)
    lon_last = (lax.axis_index("lon") == 15).astype(jnp.int32)
    mask = head_mask(BF)
    maskf = head_mask(F32)

    def arrive(p):
        in_halo[p, 0:224] = out_halo[p, 0:224]
        for copy in coming[p]:
            copy.wait_recv()
        tok[pair_rows(p), :] = dot(place_m[0:288, :], in_halo[p]).astype(BF)
        cot[pair_rows(p), :] = dot(place_m[288:576, :], in_halo[p]).astype(BF)
        project(p, tok, cot, w_qkv, w_proj_t, hat, normed, inv, q, k, v, dc)

    def attention(p, g):
        attend(p, g, lat_last, lon_last, mask, maskf, q, k, v, dc, qs, cs, pt, st, sf, df, ctx, dqkv)

    def swap_in(g):
        return core_swap(grad.at[g, 1 - core], swapped.at[g], swap_send.at[g], swap_recv.at[g])

    def sum_first(g):
        swap_in(g).wait()
        mixed[g] = (grad[g, core].astype(F32) + swapped[g].astype(F32)).astype(BF)
        scatter_first(mixed.at[g], parts.at[g], send.at[g], recv.at[g])
        for b in range(2):
            at = first_at(b)
            parts[g, b, at] = mixed[g, b, pl.ds(at * 16, 16)]

    def sum_second():
        for b in range(2):
            for g in range(2):
                drain(parts.at[g, b, pl.ds(0, 3)], recv.at[g, b])
                mixed2[b, :, g] = jnp.sum(parts[g, b].astype(F32), axis=0).astype(BF)
        scatter_second(mixed2, parts2, send.at[2], recv.at[2])
        for b in range(2):
            at = second_at(b)
            parts2[b, at] = mixed2[b, at]

    def spread_second():
        for b in range(2):
            drain(parts2.at[b, pl.ds(0, 15)], recv.at[2, b])
            final = jnp.sum(parts2[b].astype(F32), axis=0) * NORM
            total[core, b, first_at(b) * 16 + second_at(b)] = final.astype(BF)
        gather_second(total.at[core], send.at[3], recv.at[3])

    def core_out(b, i):
        part = total.at[core, b, pl.ds((first_at(b) ^ i) * 16, 16)]
        return core_swap(part, part, core_send.at[b, i], core_recv.at[b, i])

    def spread_first():
        for b in range(2):
            drain(parts2.at[b, pl.ds(0, 15)], recv.at[3, b])
            gather_first(b, total.at[core], wide_send, wide_recv)
        for b in range(2):
            core_out(b, 0).start()
        for i in (1, 3, 2):
            for b in range(2):
                drain(total.at[core, b, pl.ds(0, 16)], wide_recv.at[b, i])
                core_out(b, i).start()

    def write_half(half):
        for g in range(2):
            for b in range(2):
                if half == 0:
                    for part in range(2):
                        at = 512 * part + 256 * g + 128 * b
                        rows = slice(32 * part, 32 * part + 32)
                        gqkv[:, at : at + 128] = total[0, b, rows, g].reshape(512, 128).astype(F32)
                    continue
                at = 1024 + 256 * g + 128 * b
                gqkv[:, at : at + 128] = total[1, b, 0:32, g].reshape(512, 128).astype(F32)
                for side in range(2):
                    at = 256 * side + 128 * b
                    piece = total[1, b, 32 + 16 * side : 48 + 16 * side, g].reshape(256, 128)
                    gproj[256 * g : 256 * g + 256, at : at + 128] = piece.astype(F32)
        for copy in write_copies(half):
            copy.start()

    def write_copies(half):
        if half == 0:
            at = pl.ds(0, 1024)
            return [pltpu.make_async_copy(gqkv.at[:, at], gqkv_out.at[:, at], store.at[2])]
        at = pl.ds(1024, 512)
        return [
            pltpu.make_async_copy(gqkv.at[:, at], gqkv_out.at[:, at], store.at[3]),
            pltpu.make_async_copy(gproj, gproj_out, store.at[4]),
        ]

    def write_own():
        for half in range(2):
            @pl.when(core == half)
            def _():
                write_half(half)

    def write_other():
        for b in range(2):
            for i in range(4):
                core_out(b, i).wait()
        for half in range(2):
            @pl.when(core != half)
            def _():
                write_half(half)

    def drain_sends():
        for b in range(2):
            for g in range(2):
                drain(parts.at[g, b, pl.ds(0, 3)], send.at[g, b])
                drain(parts2.at[b, pl.ds(0, 15)], send.at[2 + g, b])
            for i in range(1, 4):
                drain(total.at[core, b, pl.ds(0, 16)], wide_send.at[b, i])

    def back(p):
        in_back[p, 0:224] = out_back[p, 0:224]
        for copy in going[p]:
            copy.wait_recv()
        for half in range(2):
            for level in range(2):
                at = 144 * ((2 * p + 1 + level) % 4)
                rows = slice(288 * half + 144 * level, 288 * half + 144 * level + 144)
                d = dot(unpack[rows, :], in_back[p]).astype(BF)
                moved[half, at : at + 144, :] = (both[p, rows, :].astype(F32) + d.astype(F32)).astype(BF)

    going = [halo(p, 1, out_back, in_back, bsend, brecv) for p in range(2)]

    def leave(p):
        finish(p, w_qkv_t, w_proj, hat, inv, ctx, dqkv, done)
        out_back[p] = dot(unplace[...], done[p]).astype(BF)
        for copy in going[p]:
            copy.start()

    arrive(0)

    @pl.loop(0, 2)
    def _(g):
        attention(0, g)

    leave(0)
    arrive(1)
    attention(1, 0)
    weight_gradients(0, normed, cot, ctx, dqkv, grad)
    swap_in(0).start()
    attention(1, 1)
    sum_first(0)
    weight_gradients(1, normed, cot, ctx, dqkv, grad)
    swap_in(1).start()
    leave(1)
    sum_first(1)
    sum_second()
    back(0)
    spread_second()
    back(1)
    outs = [pltpu.make_async_copy(moved.at[i], (output, grad_tokens)[i], store.at[i]) for i in range(2)]
    for copy in outs:
        copy.start()
    spread_first()
    write_own()
    drain_sends()
    for p in range(2):
        for copy in coming[p] + going[p]:
            copy.wait_send()
    write_other()
    for copy in outs + write_copies(0) + write_copies(1):
        copy.wait()


def block(tokens, cotangent, w_qkv, w_proj):
    hbm = pl.BlockSpec(memory_space=pl.ANY)
    dma = pltpu.SemaphoreType.DMA
    return pl.pallas_call(
        kernel,
        out_shape=(
            jax.ShapeDtypeStruct((576, 512), BF),
            jax.ShapeDtypeStruct((576, 512), BF),
            jax.ShapeDtypeStruct((512, 1536), F32),
            jax.ShapeDtypeStruct((512, 512), F32),
        ),
        in_specs=[hbm] * 8,
        out_specs=(hbm,) * 4,
        scratch_shapes=[
            pltpu.VMEM((2, 576, 512), BF),
            pltpu.VMEM((512, 1536), F32),
            pltpu.VMEM((512, 512), F32),
            pltpu.VMEM((2, 576, 512), BF),
            pltpu.VMEM((512, 1536), BF),
            pltpu.VMEM((512, 512), BF),
            pltpu.VMEM((1536, 512), BF),
            pltpu.VMEM((512, 512), BF),
            pltpu.VMEM((ROWS, 576), BF),
            pltpu.VMEM((576, ROWS), BF),
            pltpu.VMEM((ROWS, 576), BF),
            pltpu.VMEM((576, ROWS), BF),
            pltpu.VMEM((2, ROWS, 512), BF),
            pltpu.VMEM((2, ROWS, 512), BF),
            pltpu.VMEM((2, ROWS, 512), BF),
            pltpu.VMEM((2, ROWS, 512), BF),
            pltpu.VMEM((576, 512), BF),
            pltpu.VMEM((576, 512), BF),
            pltpu.VMEM((576, 512), F32),
            pltpu.VMEM((576, 512), BF),
            pltpu.VMEM((576, 128), F32),
            pltpu.VMEM((2, 576, 256), BF),
            pltpu.VMEM((2, 576, 256), BF),
            pltpu.VMEM((2, 576, 256), BF),
            pltpu.VMEM((2, 576, 256), BF),
            pltpu.VMEM((2, 1152, 256), BF),
            pltpu.VMEM((2, 1152, 256), BF),
            pltpu.VMEM((4, 144, 1152), BF),
            pltpu.VMEM((4, 144, 1152), BF),
            pltpu.VMEM((2, 144, 1152), F32),
            pltpu.VMEM((2, 144, 1152), F32),
            pltpu.VMEM((576, 512), BF),
            pltpu.VMEM((576, 1536), BF),
            pltpu.VMEM((2, 576, 512), BF),
            pltpu.VMEM((2, 2, 2, 64, 16, 128), BF),
            pltpu.VMEM((2, 2, 64, 16, 128), BF),
            pltpu.VMEM((2, 2, 64, 16, 128), BF),
            pltpu.VMEM((2, 2, 4, 16, 16, 128), BF),
            pltpu.VMEM((2, 16, 2, 16, 128), BF),
            pltpu.VMEM((2, 16, 2, 16, 128), BF),
            pltpu.VMEM((2, 2, 64, 2, 16, 128), BF),
            dma((16,)),
            dma((5,)),
            dma((2,)),
            dma((2,)),
            dma((4, 2)),
            dma((4, 2)),
            dma((2, 4)),
            dma((2, 4)),
            dma((2, 4)),
            dma((2, 4)),
            dma((2, 3)),
            dma((2, 3)),
            dma((2, 3)),
            dma((2, 3)),
        ],
        compiler_params=pltpu.CompilerParams(
            vmem_limit_bytes=56 * 2**20, collective_id=0, has_side_effects=True
        ),
        name="window_block",
    )(tokens, cotangent, w_qkv, w_proj, *orders())


def body(tokens, cotangent, w_qkv, w_proj):
    shape = tokens.shape
    output, grad_tokens, gqkv, gproj = block(
        tokens.reshape(576, 512), cotangent.reshape(576, 512), w_qkv, w_proj
    )
    return (output.reshape(shape), grad_tokens.reshape(shape), gqkv, gproj)


def solution(mesh):
    spec = P(None, "lat", "lon", None)
    return jax.shard_map(
        body,
        mesh=mesh,
        in_specs=(spec, spec, P(), P()),
        out_specs=(spec, spec, P(), P()),
        check_vma=False,
    )
```

time: 79 us -> 78.6 us (level)
  local copies, waits for them, and re-layouts: 1.67 us -> 8.66 us
  other arithmetic: 4.64 us -> 0 us
  Pallas kernels: 71.9 us -> 69.1 us
    unnamed x8 -> x6, local copies, waits for them, and re-layouts: 1.67 us -> 8.66 us
    convert_element_type x2 -> x0, other arithmetic: 4.64 us -> none  [the longest x1 3.54 us: body(): gqkv.astype(F32)]
    pallas_call x1, Pallas kernels: 71.9 us -> 69.1 us  [block(): pl.pallas_call(kernel, out_shape=(jax.ShapeDtypeStruct((576, 512), BF), j...]
where the time goes in v4:
time: 78.6 us; the launch traced here: 78.4 us
  Pallas kernels  69.1 us (88%)
  local copies, waits for them, and re-layouts  8.66 us (11%)
    pallas_call x1, Pallas kernels, block(): pl.pallas_call(kernel, out_shape=(jax.ShapeDtypeStruct((576, 512), BF), j...  69.1 us
    unnamed x6, local copies, waits for them, and re-layouts  8.66 us

profile of v4, /device:TPU:1, one launch (start us, length us, event | category | flops | bytes accessed | tf_op | source)
XLA Modules:
  0.0 78.4 jit_solution(15656066182976764461)
XLA Ops:
  0.6 69.1 %window_block.1 = (bf16[576,512]{1,0:T(8,128)(2,1)}, bf16[576,512]{1,0:T(8,128)(2,1)}, f32[512,1536]{1,0:T(8,128)}, f32[512,512]{1,0:T(8,128)}) custom-call(bf16[576,512]{1,0:T(8,128)(2,1)} %bitcast.4, bf16[576,512]{1,0:T(8,128)(2,1)} %bitcast.5, bf16[512,1536]{1,0:T(8,128)(2,1)} %w_qkv_in.1, bf16[512,512]{1,0:T(8,128)(2,1)} %w_proj_in.1, ...), custom_call_target="tpu_custom_call" | custom-call | tf_op jit(solution)/shard_map/window_block/pallas_call | solution.py:538
  69.8 1.9 %copy.16 = bf16[4,6,24,512]{3,2,1,0:T(8,128)(2,1)} copy(bf16[4,6,24,512]{3,2,1,0:T(8,128)(2,1)} %bitcast.7) | data formatting | bytes 1179648
  71.7 1.9 %copy.17 = bf16[4,6,24,512]{3,2,1,0:T(8,128)(2,1)} copy(bf16[4,6,24,512]{3,2,1,0:T(8,128)(2,1)} %bitcast.6) | data formatting | bytes 1179648
  73.6 0.0 copy-start
  73.6 3.8 %copy.18 = f32[512,1536]{1,0:T(8,128)} copy(f32[512,1536]{1,0:T(8,128)} %get-tuple-element.18) | data formatting | bytes 6291456
  77.4 0.0 copy-done
  77.5 1.0 %copy.19 = f32[512,512]{1,0:T(8,128)} copy(f32[512,512]{1,0:T(8,128)S(1)} %copy-done) | data formatting | bytes 2097152
Async XLA Ops:
  73.6 3.8 %copy-start = (f32[512,512]{1,0:T(8,128)S(1)}, f32[512,512]{1,0:T(8,128)}, u32[]{:S(2)}) copy-start(f32[512,512]{1,0:T(8,128)} %get-tuple-element.19) | copy-start | bytes 3145732

commit v5 on v4

--- a/solution.py
+++ b/solution.py
@@ -319,10 +319,10 @@
 
 def kernel(
     tokens, cotangent, w_qkv_in, w_proj_in, pack_in, place_in, unplace_in, unpack_in,
-    output, grad_tokens, gqkv_out, gproj_out,
-    moved, gqkv, gproj, both, w_qkv, w_proj, w_qkv_t, w_proj_t, pack, place_m, unplace, unpack, out_halo, in_halo, out_back, in_back,
+    output, grad_tokens, gqkv, gproj,
+    both, w_qkv, w_proj, w_qkv_t, w_proj_t, pack, place_m, unplace, unpack, out_halo, in_halo, out_back, in_back,
     tok, cot, hat, normed, inv, q, k, v, dc, qs, cs, pt, st, sf, df, ctx, dqkv, done,
-    grad, swapped, mixed, parts, mixed2, parts2, total, load, store, swap_send, swap_recv, send, recv, core_send, core_recv, wide_send, wide_recv, hsend, hrecv, bsend, brecv,
+    grad, swapped, mixed, parts, mixed2, parts2, total, load, swap_send, swap_recv, send, recv, core_send, core_recv, wide_send, wide_recv, hsend, hrecv, bsend, brecv,
 ):
     x, y, z, core = place()
     greet()
@@ -420,6 +420,7 @@
         for b in range(2):
             drain(parts2.at[b, pl.ds(0, 15)], recv.at[3, b])
             gather_first(b, total.at[core], wide_send, wide_recv)
+        send_back(1)
         for b in range(2):
             core_out(b, 0).start()
         for i in (1, 3, 2):
@@ -442,18 +443,6 @@
                     at = 256 * side + 128 * b
                     piece = total[1, b, 32 + 16 * side : 48 + 16 * side, g].reshape(256, 128)
                     gproj[256 * g : 256 * g + 256, at : at + 128] = piece.astype(F32)
-        for copy in write_copies(half):
-            copy.start()
-
-    def write_copies(half):
-        if half == 0:
-            at = pl.ds(0, 1024)
-            return [pltpu.make_async_copy(gqkv.at[:, at], gqkv_out.at[:, at], store.at[2])]
-        at = pl.ds(1024, 512)
-        return [
-            pltpu.make_async_copy(gqkv.at[:, at], gqkv_out.at[:, at], store.at[3]),
-            pltpu.make_async_copy(gproj, gproj_out, store.at[4]),
-        ]
 
     def write_own():
         for half in range(2):
@@ -482,18 +471,20 @@
         in_back[p, 0:224] = out_back[p, 0:224]
         for copy in going[p]:
             copy.wait_recv()
-        for half in range(2):
+        for half, out in enumerate((output, grad_tokens)):
             for level in range(2):
                 at = 144 * ((2 * p + 1 + level) % 4)
                 rows = slice(288 * half + 144 * level, 288 * half + 144 * level + 144)
                 d = dot(unpack[rows, :], in_back[p]).astype(BF)
-                moved[half, at : at + 144, :] = (both[p, rows, :].astype(F32) + d.astype(F32)).astype(BF)
+                out[at : at + 144, :] = (both[p, rows, :].astype(F32) + d.astype(F32)).astype(BF)
 
     going = [halo(p, 1, out_back, in_back, bsend, brecv) for p in range(2)]
 
     def leave(p):
         finish(p, w_qkv_t, w_proj, hat, inv, ctx, dqkv, done)
         out_back[p] = dot(unplace[...], done[p]).astype(BF)
+
+    def send_back(p):
         for copy in going[p]:
             copy.start()
 
@@ -504,6 +495,7 @@
         attention(0, g)
 
     leave(0)
+    send_back(0)
     arrive(1)
     attention(1, 0)
     weight_gradients(0, normed, cot, ctx, dqkv, grad)
@@ -512,24 +504,20 @@
     sum_first(0)
     weight_gradients(1, normed, cot, ctx, dqkv, grad)
     swap_in(1).start()
-    leave(1)
+    finish(1, w_qkv_t, w_proj, hat, inv, ctx, dqkv, done)
     sum_first(1)
+    out_back[1] = dot(unplace[...], done[1]).astype(BF)
+    back(0)
     sum_second()
-    back(0)
     spread_second()
-    back(1)
-    outs = [pltpu.make_async_copy(moved.at[i], (output, grad_tokens)[i], store.at[i]) for i in range(2)]
-    for copy in outs:
-        copy.start()
     spread_first()
     write_own()
+    back(1)
     drain_sends()
     for p in range(2):
         for copy in coming[p] + going[p]:
             copy.wait_send()
     write_other()
-    for copy in outs + write_copies(0) + write_copies(1):
-        copy.wait()
 
 
 def block(tokens, cotangent, w_qkv, w_proj):
@@ -544,11 +532,8 @@
             jax.ShapeDtypeStruct((512, 512), F32),
         ),
         in_specs=[hbm] * 8,
-        out_specs=(hbm,) * 4,
+        out_specs=(pl.BlockSpec(memory_space=pltpu.VMEM),) * 4,
         scratch_shapes=[
-            pltpu.VMEM((2, 576, 512), BF),
-            pltpu.VMEM((512, 1536), F32),
-            pltpu.VMEM((512, 512), F32),
             pltpu.VMEM((2, 576, 512), BF),
             pltpu.VMEM((512, 1536), BF),
             pltpu.VMEM((512, 512), BF),
@@ -588,7 +573,6 @@
             pltpu.VMEM((2, 16, 2, 16, 128), BF),
             pltpu.VMEM((2, 2, 64, 2, 16, 128), BF),
             dma((16,)),
-            dma((5,)),
             dma((2,)),
             dma((2,)),
             dma((4, 2)),
@@ -603,17 +587,32 @@
             dma((2, 3)),
         ],
         compiler_params=pltpu.CompilerParams(
-            vmem_limit_bytes=56 * 2**20, collective_id=0, has_side_effects=True
+            vmem_limit_bytes=50 * 2**20, collective_id=0, has_side_effects=True
         ),
         name="window_block",
     )(tokens, cotangent, w_qkv, w_proj, *orders())
 
 
+def hand_over(*refs):
+    copies = [pltpu.make_async_copy(refs[i], refs[4 + i], refs[8].at[i]) for i in range(4)]
+    for copy in copies:
+        copy.start()
+    for copy in copies:
+        copy.wait()
+
+
 def body(tokens, cotangent, w_qkv, w_proj):
     shape = tokens.shape
-    output, grad_tokens, gqkv, gproj = block(
-        tokens.reshape(576, 512), cotangent.reshape(576, 512), w_qkv, w_proj
-    )
+    results = block(tokens.reshape(576, 512), cotangent.reshape(576, 512), w_qkv, w_proj)
+    hbm = pl.BlockSpec(memory_space=pl.ANY)
+    output, grad_tokens, gqkv, gproj = pl.pallas_call(
+        hand_over,
+        out_shape=tuple(jax.ShapeDtypeStruct(r.shape, r.dtype) for r in results),
+        in_specs=[hbm] * 4,
+        out_specs=(hbm,) * 4,
+        scratch_shapes=[pltpu.SemaphoreType.DMA((4,))],
+        name="hand_over",
+    )(*results)
     return (output.reshape(shape), grad_tokens.reshape(shape), gqkv, gproj)
 
 

time: 78.6 us -> 242 us (3.08)
  Pallas kernels: 69.1 us -> 235 us
  local copies, waits for them, and re-layouts: 8.66 us -> 5.91 us
    pallas_call x0 -> x1, Pallas kernels: none -> 164 us  [body(): pl.pallas_call(hand_over, out_shape=tuple((jax.ShapeDtypeStruct(r.shape,...]
    unnamed x6 -> x12, local copies, waits for them, and re-layouts: 8.66 us -> 5.91 us
where the time goes in v5:
time: 242 us
  Pallas kernels  235 us (97%)
  local copies, waits for them, and re-layouts  5.91 us (2%)
    pallas_call x1, Pallas kernels, body(): pl.pallas_call(hand_over, out_shape=tuple((jax.ShapeDtypeStruct(r.shape,...  164 us
    pallas_call x1, Pallas kernels, block(): pl.pallas_call(kernel, out_shape=(jax.ShapeDtypeStruct((576, 512), BF), j...  71.4 us
    unnamed x12, local copies, waits for them, and re-layouts  5.91 us

profile of v5, /device:TPU:1, one launch (start us, length us, event | category | flops | bytes accessed | tf_op | source)
XLA Modules:
  0.0 242.1 jit_solution(12264416913570600113)
XLA Ops:
  0.6 0.0 copy-start
  0.6 1.1 copy-done
  1.8 0.0 copy-start.1
  1.8 1.1 copy-done.1
  2.8 0.0 copy-start.2
  2.8 1.1 copy-done.2
  3.9 0.0 copy-start.5
  3.9 1.0 copy-done.5
  4.9 71.4 %window_block.1 = (bf16[576,512]{1,0:T(8,128)(2,1)S(1)}, bf16[576,512]{1,0:T(8,128)(2,1)S(1)}, f32[512,1536]{1,0:T(8,128)}, f32[512,512]{1,0:T(8,128)}) custom-call(bf16[576,512]{1,0:T(8,128)(2,1)S(1)} %bitcast.4, bf16[576,512]{1,0:T(8,128)(2,1)S(1)} %bitcast.5, bf16[512,1536]{1,0:T(8,128)(2,1)} %w_qkv_in.1, bf16[512,512]{1,0:T(8,128)(2,1)S(1)} %copy-done.5, ...), custom_call_target="tpu_custom_call" | custom-call | tf_op jit(solution)/shard_map/window_block/pallas_call | solution.py:526
  76.3 0.0 copy-start.3
  76.3 0.8 copy-done.3
  77.1 0.0 copy-start.4
  77.1 0.8 copy-done.4
  78.0 163.9 %hand_over.1 = (bf16[576,512]{1,0:T(8,128)(2,1)}, bf16[576,512]{1,0:T(8,128)(2,1)}, f32[512,1536]{1,0:T(8,128)}, f32[512,512]{1,0:T(8,128)}) custom-call(bf16[576,512]{1,0:T(8,128)(2,1)} %copy-done.3, bf16[576,512]{1,0:T(8,128)(2,1)} %copy-done.4, f32[512,1536]{1,0:T(8,128)} %get-tuple-element.14.refs_2_, f32[512,512]{1,0:T(8,128)} %get-tuple-element.15.refs_3_), custom_call_target="tpu_custom_call" | custom-call | tf_op jit(solution)/shard_map/hand_over/pallas_call | solution.py:608
Async XLA Ops:
  0.6 1.1 copy-start
  1.8 1.1 copy-start.1
  2.8 1.1 copy-start.2
  3.9 1.0 copy-start.5
  76.3 0.8 copy-start.3
  77.1 0.8 copy-start.4

commit v6 on v5

--- a/solution.py
+++ b/solution.py
@@ -319,10 +319,10 @@
 
 def kernel(
     tokens, cotangent, w_qkv_in, w_proj_in, pack_in, place_in, unplace_in, unpack_in,
-    output, grad_tokens, gqkv, gproj,
-    both, w_qkv, w_proj, w_qkv_t, w_proj_t, pack, place_m, unplace, unpack, out_halo, in_halo, out_back, in_back,
+    output, grad_tokens, total_out,
+    moved, both, w_qkv, w_proj, w_qkv_t, w_proj_t, pack, place_m, unplace, unpack, out_halo, in_halo, out_back, in_back,
     tok, cot, hat, normed, inv, q, k, v, dc, qs, cs, pt, st, sf, df, ctx, dqkv, done,
-    grad, swapped, mixed, parts, mixed2, parts2, total, load, swap_send, swap_recv, send, recv, core_send, core_recv, wide_send, wide_recv, hsend, hrecv, bsend, brecv,
+    grad, swapped, mixed, parts, mixed2, parts2, total, load, store, swap_send, swap_recv, send, recv, core_send, core_recv, wide_send, wide_recv, hsend, hrecv, bsend, brecv,
 ):
     x, y, z, core = place()
     greet()
@@ -428,36 +428,12 @@
                 drain(total.at[core, b, pl.ds(0, 16)], wide_recv.at[b, i])
                 core_out(b, i).start()
 
-    def write_half(half):
-        for g in range(2):
-            for b in range(2):
-                if half == 0:
-                    for part in range(2):
-                        at = 512 * part + 256 * g + 128 * b
-                        rows = slice(32 * part, 32 * part + 32)
-                        gqkv[:, at : at + 128] = total[0, b, rows, g].reshape(512, 128).astype(F32)
-                    continue
-                at = 1024 + 256 * g + 128 * b
-                gqkv[:, at : at + 128] = total[1, b, 0:32, g].reshape(512, 128).astype(F32)
-                for side in range(2):
-                    at = 256 * side + 128 * b
-                    piece = total[1, b, 32 + 16 * side : 48 + 16 * side, g].reshape(256, 128)
-                    gproj[256 * g : 256 * g + 256, at : at + 128] = piece.astype(F32)
-
-    def write_own():
-        for half in range(2):
-            @pl.when(core == half)
-            def _():
-                write_half(half)
-
-    def write_other():
-        for b in range(2):
-            for i in range(4):
-                core_out(b, i).wait()
-        for half in range(2):
-            @pl.when(core != half)
-            def _():
-                write_half(half)
+    def store_half(half, i):
+        return pltpu.make_async_copy(total.at[half], total_out.at[half], store.at[2 + i])
+
+    def store_moved():
+        outs = (output, grad_tokens)
+        return [pltpu.make_async_copy(moved.at[i], outs[i], store.at[i]) for i in range(2)]
 
     def drain_sends():
         for b in range(2):
@@ -471,12 +447,12 @@
         in_back[p, 0:224] = out_back[p, 0:224]
         for copy in going[p]:
             copy.wait_recv()
-        for half, out in enumerate((output, grad_tokens)):
+        for half in range(2):
             for level in range(2):
                 at = 144 * ((2 * p + 1 + level) % 4)
                 rows = slice(288 * half + 144 * level, 288 * half + 144 * level + 144)
                 d = dot(unpack[rows, :], in_back[p]).astype(BF)
-                out[at : at + 144, :] = (both[p, rows, :].astype(F32) + d.astype(F32)).astype(BF)
+                moved[half, at : at + 144, :] = (both[p, rows, :].astype(F32) + d.astype(F32)).astype(BF)
 
     going = [halo(p, 1, out_back, in_back, bsend, brecv) for p in range(2)]
 
@@ -511,13 +487,20 @@
     sum_second()
     spread_second()
     spread_first()
-    write_own()
+    store_half(core, 0).start()
     back(1)
+    for copy in store_moved():
+        copy.start()
     drain_sends()
     for p in range(2):
         for copy in coming[p] + going[p]:
             copy.wait_send()
-    write_other()
+    for b in range(2):
+        for i in range(4):
+            core_out(b, i).wait()
+    store_half(1 - core, 1).start()
+    for copy in store_moved() + [store_half(core, 0), store_half(1 - core, 1)]:
+        copy.wait()
 
 
 def block(tokens, cotangent, w_qkv, w_proj):
@@ -528,12 +511,12 @@
         out_shape=(
             jax.ShapeDtypeStruct((576, 512), BF),
             jax.ShapeDtypeStruct((576, 512), BF),
-            jax.ShapeDtypeStruct((512, 1536), F32),
-            jax.ShapeDtypeStruct((512, 512), F32),
+            jax.ShapeDtypeStruct((2, 2, 64, 2, 16, 128), BF),
         ),
         in_specs=[hbm] * 8,
-        out_specs=(pl.BlockSpec(memory_space=pltpu.VMEM),) * 4,
+        out_specs=(hbm,) * 3,
         scratch_shapes=[
+            pltpu.VMEM((2, 576, 512), BF),
             pltpu.VMEM((2, 576, 512), BF),
             pltpu.VMEM((512, 1536), BF),
             pltpu.VMEM((512, 512), BF),
@@ -573,6 +556,7 @@
             pltpu.VMEM((2, 16, 2, 16, 128), BF),
             pltpu.VMEM((2, 2, 64, 2, 16, 128), BF),
             dma((16,)),
+            dma((4,)),
             dma((2,)),
             dma((2,)),
             dma((4, 2)),
@@ -587,17 +571,50 @@
             dma((2, 3)),
         ],
         compiler_params=pltpu.CompilerParams(
-            vmem_limit_bytes=50 * 2**20, collective_id=0, has_side_effects=True
+            vmem_limit_bytes=56 * 2**20, collective_id=0, has_side_effects=True
         ),
         name="window_block",
     )(tokens, cotangent, w_qkv, w_proj, *orders())
 
 
-def hand_over(*refs):
-    copies = [pltpu.make_async_copy(refs[i], refs[4 + i], refs[8].at[i]) for i in range(4)]
-    for copy in copies:
+def hand_over(moved_a, moved_b, total_in, out_a, out_b, gqkv_out, gproj_out, moved, total, gqkv, gproj, load, store):
+    loads = [
+        pltpu.make_async_copy(total_in.at[0], total.at[0], load.at[0]),
+        pltpu.make_async_copy(total_in.at[1], total.at[1], load.at[1]),
+        pltpu.make_async_copy(moved_a, moved.at[0], load.at[2]),
+        pltpu.make_async_copy(moved_b, moved.at[1], load.at[3]),
+    ]
+    for copy in loads:
         copy.start()
-    for copy in copies:
+    stores = []
+
+    def write(src, dst):
+        copy = pltpu.make_async_copy(src, dst, store.at[len(stores)])
+        copy.start()
+        stores.append(copy)
+
+    for part in range(3):
+        if part != 1:
+            loads[part // 2].wait()
+        for g in range(2):
+            for b in range(2):
+                at = 512 * part + 256 * g + 128 * b
+                rows = slice(32 * (part % 2), 32 * (part % 2) + 32)
+                gqkv[:, at : at + 128] = total[part // 2, b, rows, g].reshape(512, 128).astype(F32)
+        at = pl.ds(512 * part, 512)
+        write(gqkv.at[:, at], gqkv_out.at[:, at])
+    for g in range(2):
+        for b in range(2):
+            for side in range(2):
+                at = 256 * side + 128 * b
+                piece = total[1, b, 32 + 16 * side : 48 + 16 * side, g].reshape(256, 128)
+                gproj[256 * g : 256 * g + 256, at : at + 128] = piece.astype(F32)
+    write(gproj, gproj_out)
+    loads[2].wait()
+    write(moved.at[0], out_a)
+    loads[3].wait()
+    write(moved.at[1], out_b)
+    for copy in stores:
         copy.wait()
 
 
@@ -607,10 +624,23 @@
     hbm = pl.BlockSpec(memory_space=pl.ANY)
     output, grad_tokens, gqkv, gproj = pl.pallas_call(
         hand_over,
-        out_shape=tuple(jax.ShapeDtypeStruct(r.shape, r.dtype) for r in results),
-        in_specs=[hbm] * 4,
+        out_shape=(
+            jax.ShapeDtypeStruct((576, 512), BF),
+            jax.ShapeDtypeStruct((576, 512), BF),
+            jax.ShapeDtypeStruct((512, 1536), F32),
+            jax.ShapeDtypeStruct((512, 512), F32),
+        ),
+        in_specs=[hbm] * 3,
         out_specs=(hbm,) * 4,
-        scratch_shapes=[pltpu.SemaphoreType.DMA((4,))],
+        scratch_shapes=[
+            pltpu.VMEM((2, 576, 512), BF),
+            pltpu.VMEM((2, 2, 64, 2, 16, 128), BF),
+            pltpu.VMEM((512, 1536), F32),
+            pltpu.VMEM((512, 512), F32),
+            pltpu.SemaphoreType.DMA((4,)),
+            pltpu.SemaphoreType.DMA((6,)),
+        ],
+        compiler_params=pltpu.CompilerParams(vmem_limit_bytes=56 * 2**20),
         name="hand_over",
     )(*results)
     return (output.reshape(shape), grad_tokens.reshape(shape), gqkv, gproj)

time: 242 us -> 74.3 us (0.31)
  Pallas kernels: 235 us -> 73.3 us
  local copies, waits for them, and re-layouts: 5.91 us -> 0 us
    pallas_call x1, Pallas kernels: 164 us -> 3.82 us  [body(): pl.pallas_call(hand_over, out_shape=(jax.ShapeDtypeStruct((576, 512), BF)...]
    unnamed x12 -> x0, local copies, waits for them, and re-layouts: 5.91 us -> none
where the time goes in v6:
time: 74.3 us; the launch traced here: 74.1 us
  Pallas kernels  73.3 us (99%)
  between operations  0.8 us (1%)
    pallas_call x1, Pallas kernels, block(): pl.pallas_call(kernel, out_shape=(jax.ShapeDtypeStruct((576, 512), BF), j...  69.5 us
    pallas_call x1, Pallas kernels, body(): pl.pallas_call(hand_over, out_shape=(jax.ShapeDtypeStruct((576, 512), BF)...  3.82 us

profile of v6, /device:TPU:1, one launch (start us, length us, event | category | flops | bytes accessed | tf_op | source)
XLA Modules:
  0.0 74.1 jit_solution(3919497109829672768)
XLA Ops:
  0.6 69.5 %window_block.1 = (bf16[576,512]{1,0:T(8,128)(2,1)}, bf16[576,512]{1,0:T(8,128)(2,1)}, bf16[2,2,64,2,16,128]{5,4,3,2,1,0:T(8,128)(2,1)}) custom-call(bf16[576,512]{1,0:T(8,128)(2,1)} %bitcast.4, bf16[576,512]{1,0:T(8,128)(2,1)} %bitcast.5, bf16[512,1536]{1,0:T(8,128)(2,1)} %w_qkv_in.1, bf16[512,512]{1,0:T(8,128)(2,1)} %w_proj_in.1, ...), custom_call_target="tpu_custom_call" | custom-call | tf_op jit(solution)/shard_map/window_block/pallas_call | solution.py:509
  70.2 3.8 %hand_over.1 = (bf16[576,512]{1,0:T(8,128)(2,1)}, bf16[576,512]{1,0:T(8,128)(2,1)}, f32[512,1536]{1,0:T(8,128)}, f32[512,512]{1,0:T(8,128)}) custom-call(bf16[576,512]{1,0:T(8,128)(2,1)} %get-tuple-element.11.moved_a, bf16[576,512]{1,0:T(8,128)(2,1)} %get-tuple-element.12.moved_b, bf16[2,2,64,2,16,128]{5,4,3,2,1,0:T(8,128)(2,1)} %get-tuple-element.13.total_in), custom_call_target="tpu_custom_call" | custom-call | tf_op jit(solution)/shard_map/hand_over/pallas_call | solution.py:625

commit v7 on v6

--- a/solution.py
+++ b/solution.py
@@ -16,33 +16,35 @@
 TN = (((0,), (0,)), ((), ()))
 MESH = pl.DeviceIdType.MESH
 
-STARTS = (0, 224, 448, 528)
 ROWS = 608
-SECTIONS = ((224, 224), (448, 80), (528, 80))
+KEPT = ((0, 144), (288, 80))
+SENT = (((144, 144, 1, 0),), ((368, 80, 1, 0), (448, 80, 0, 1), (528, 80, 1, 1)))
+SPAN = (slice(0, 288), slice(288, 608))
 
 
 def section_row(array, level, row, col):
-    section = (2 if col < 6 else 0) + (1 if row < 3 else 0)
-    width, first = (18, 6) if col >= 6 else (6, 0)
-    at = (level * 3 + row % 3) * width + col - first
-    return STARTS[section] + array * 6 * width + at
+    line = level * 3 + row % 3
+    if 6 <= col < 18:
+        return (144 if row < 3 else 0) + array * 72 + line * 12 + col - 6
+    start = (448 if col < 6 else 288) + (80 if row < 3 else 0)
+    return start + array * 36 + line * 6 + col % 18
 
 
 def orders():
     pack = np.zeros((ROWS, 576), np.float32)
-    place = np.zeros((576, ROWS), np.float32)
+    place = np.zeros((2, 288, ROWS), np.float32)
     for array in range(2):
         for level in range(2):
             for row in range(6):
                 for col in range(24):
                     at = array * 288 + level * 144 + row * 24 + col
                     pack[section_row(array, level, row, col), at] = 1
-            for row in range(6):
-                for col in range(24):
-                    at = array * 288 + col // 12 * 144 + level * 72 + row * 12 + col % 12
+                    loc, c = col // 12, col % 12
+                    at = array * 144 + level * 72 + row * 12 + c
                     source = section_row(array, level, (row + 3) % 6, (col + 6) % 24)
-                    place[at, source] = 1
-    return [jnp.asarray(m, BF) for m in (pack, place, place.T, pack.T)]
+                    place[loc, at, source] = 1
+    place = [place[loc][:, SPAN[loc]] for loc in range(2)]
+    return [jnp.asarray(m, BF) for m in (pack, *place, place[0].T, place[1].T, pack.T)]
 
 
 def dot(a, b, dims=NN):
@@ -63,14 +65,14 @@
     return slice(288 * p, 288 * p + 288)
 
 
-def project(p, tok, cot, w_qkv, w_proj_t, hat, normed, inv, q, k, v, dc):
-    rows = pair_rows(p)
+def project(w, tok, cot, w_qkv, w_proj_t, hat, normed, inv, q, k, v, dc):
+    rows = slice(144 * w, 144 * w + 144)
     x = tok[rows, :].astype(F32)
     x = x - jnp.mean(x, axis=1, keepdims=True)
     scale = lax.rsqrt(jnp.mean(x * x, axis=1, keepdims=True) + 1e-05)
     x = x * scale
     hat[rows, :] = x
-    inv[rows, :] = jnp.broadcast_to(scale, (288, 128))
+    inv[rows, :] = jnp.broadcast_to(scale, (144, 128))
     x = x.astype(BF)
     normed[rows, :] = x
     for g in range(2):
@@ -92,67 +94,68 @@
     return [(key_rows(p, c), slice(128 * c, 128 * d)) for c, d in ((0, 4), (4, 5), (5, 9))]
 
 
-def attend(p, g, lat_last, lon_last, mask, maskf, q, k, v, dc, qs, cs, pt, st, sf, df, ctx, dqkv):
-    def rows(i):
-        return slice(144 * (2 * p + i), 144 * (2 * p + i) + 144)
-
-    def scores(i):
-        first = 144 * (2 * p + i)
-        keys, vals = k[g, rows(i), :], v[g, rows(i), :]
+def attend(w, groups, lat_last, lon_last, mask, maskf, q, k, v, dc, qs, cs, pt, st, sf, df, ctx, dqkv):
+    p = w // 2
+    first = 144 * w
+    rows = slice(first, first + 144)
+    klab, qlab = labels(w, lat_last, lon_last)
+
+    def scores(g):
+        keys, vals = k[g, rows, :], v[g, rows, :]
         for c in range(9):
             at = slice(128 * c, 128 * c + 128)
             q16 = q[g, first + 16 * c : first + 16 * c + 16, :]
             d16 = dc[g, first + 16 * c : first + 16 * c + 16, :]
-            qs[i, at, :] = jnp.concatenate([q16] * 8, axis=0) * mask
-            cs[i, at, :] = jnp.concatenate([d16] * 8, axis=0) * mask
+            qs[g, at, :] = jnp.concatenate([q16] * 8, axis=0) * mask
+            cs[g, at, :] = jnp.concatenate([d16] * 8, axis=0) * mask
         for kr, at in spans(p):
-            sf[i, kr, at] = dot(keys[kr], qs[i, at, :], NT)
-            df[i, kr, at] = dot(vals[kr], cs[i, at, :], NT)
-
-    def softmax(i):
-        klab, qlab = labels(2 * p + i, lat_last, lon_last)
+            sf[g, kr, at] = dot(keys[kr], qs[g, at, :], NT)
+            df[g, kr, at] = dot(vals[kr], cs[g, at, :], NT)
+
+    def softmax(g):
         for c in range(9):
             at = slice(128 * c, 128 * c + 128)
             kr = key_rows(p, c)
-            s = jnp.where(klab[kr] == qlab[c], sf[i, kr, at], -1e30)
+            s = jnp.where(klab[kr] == qlab[c], sf[g, kr, at], -1e30)
             e = jnp.exp2((s - jnp.max(s, axis=0, keepdims=True)) * EXP2)
             prob = e * (1.0 / jnp.sum(e, axis=0, keepdims=True))
-            pt[2 * p + i, kr, at] = prob.astype(BF)
-            dp = df[i, kr, at]
+            pt[2 * p + g, kr, at] = prob.astype(BF)
+            dp = df[g, kr, at]
             inner = jnp.sum(prob * dp, axis=0, keepdims=True)
-            st[2 * p + i, kr, at] = ((prob * SCALE) * (dp - inner)).astype(BF)
-
-    def fold(m, i, ref):
-        out = [dot(m[2 * p + i, kr, at], ref[g, rows(i), :][kr], TN) for kr, at in spans(p)]
+            st[2 * p + g, kr, at] = ((prob * SCALE) * (dp - inner)).astype(BF)
+
+    def fold(m, g, ref):
+        out = [dot(m[2 * p + g, kr, at], ref[g, rows, :][kr], TN) for kr, at in spans(p)]
         out = jnp.concatenate(out, axis=0) if len(out) > 1 else out[0]
         out = out.reshape(9, 8, 16, 256) * maskf.reshape(1, 8, 16, 256)
         return jnp.sum(out, axis=1).reshape(144, 256).astype(BF)
 
-    def columns(part):
-        return pl.ds(pl.multiple_of(768 * g + 256 * part, 256), 256)
-
-    def results(i):
-        ctx[rows(i), pl.ds(pl.multiple_of(256 * g, 256), 256)] = fold(pt, i, v)
-        dqkv[rows(i), columns(0)] = fold(st, i, k)
-        dqkv[rows(i), columns(1)] = dot(st[2 * p + i], qs[i]).astype(BF)
-        dqkv[rows(i), columns(2)] = dot(pt[2 * p + i], cs[i]).astype(BF)
-
-    scores(0)
-    scores(1)
-    softmax(0)
-    results(0)
-    softmax(1)
-    results(1)
+    def results(g):
+        at = 768 * g
+        ctx[rows, 256 * g : 256 * g + 256] = fold(pt, g, v)
+        dqkv[rows, at : at + 256] = fold(st, g, k)
+        dqkv[rows, at + 256 : at + 512] = dot(st[2 * p + g], qs[g]).astype(BF)
+        dqkv[rows, at + 512 : at + 768] = dot(pt[2 * p + g], cs[g]).astype(BF)
+
+    for g in groups:
+        scores(g)
+    for g in groups:
+        softmax(g)
+        results(g)
 
 
 def finish(p, w_qkv_t, w_proj, hat, inv, ctx, dqkv, done):
     rows = pair_rows(p)
-    done[p, 0:288, :] = dot(ctx[rows, :], w_proj[...]).astype(BF)
+    a = dot(ctx[rows, :], w_proj[...]).astype(BF)
     d = dot(dqkv[rows, :], w_qkv_t[...])
     h = hat[rows, :]
     d = d - jnp.mean(d, axis=1, keepdims=True) - h * jnp.mean(d * h, axis=1, keepdims=True)
     scale = jnp.concatenate([inv[rows, :]] * 4, axis=1)
-    done[p, 288:576, :] = (d * scale).astype(BF)
+    d = (d * scale).astype(BF)
+    for i in range(2):
+        own = slice(144 * i, 144 * i + 144)
+        done[2 * p + i, 0:144, :] = a[own]
+        done[2 * p + i, 144:288, :] = d[own]
 
 
 def labels(w, lat_last, lon_last):
@@ -249,14 +252,14 @@
     pl.semaphore_wait(pltpu.get_barrier_semaphore(), 43)
 
 
-def halo(p, step, src, dst, send, recv):
+def halo(w, step, src, dst, send, recv):
+    p, loc = w // 2, w % 2
     copies = []
-    for s, (at, count) in enumerate(SECTIONS):
-        lat_step, lon_step = ((step, 0), (0, step), (step, step))[s]
+    for s, (at, count, lat_step, lon_step) in enumerate(SENT[loc]):
         copies.append(pltpu.make_async_remote_copy(
             src_ref=src.at[p, pl.ds(at, count)], dst_ref=dst.at[p, pl.ds(at, count)],
-            send_sem=send.at[p, s], recv_sem=recv.at[p, s],
-            device_id=beside(lat_step, lon_step), device_id_type=MESH,
+            send_sem=send.at[w, s], recv_sem=recv.at[w, s],
+            device_id=beside(step * lat_step, step * lon_step), device_id_type=MESH,
         ))
     return copies
 
@@ -318,9 +321,9 @@
 
 
 def kernel(
-    tokens, cotangent, w_qkv_in, w_proj_in, pack_in, place_in, unplace_in, unpack_in,
+    tokens, cotangent, w_qkv_in, w_proj_in, pack_in, place_0, place_1, unplace_0, unplace_1, unpack_in,
     output, grad_tokens, total_out,
-    moved, both, w_qkv, w_proj, w_qkv_t, w_proj_t, pack, place_m, unplace, unpack, out_halo, in_halo, out_back, in_back,
+    moved, both, w_qkv, w_proj, w_qkv_t, w_proj_t, pack, place_a, place_b, unplace_a, unplace_b, unpack, out_halo, in_halo, out_back, in_back,
     tok, cot, hat, normed, inv, q, k, v, dc, qs, cs, pt, st, sf, df, ctx, dqkv, done,
     grad, swapped, mixed, parts, mixed2, parts2, total, load, store, swap_send, swap_recv, send, recv, core_send, core_recv, wide_send, wide_recv, hsend, hrecv, bsend, brecv,
 ):
@@ -342,21 +345,28 @@
                 )
     fetch(pack_in, pack)
     early = len(loads)
-    fetch(place_in, place_m)
+    fetch(place_0, place_a)
+    fetch(place_1, place_b)
     fetch(w_qkv_in, w_qkv)
     fetch(w_proj_in, w_proj)
-    fetch(unplace_in, unplace)
+    fetch(unplace_0, unplace_a)
+    fetch(unplace_1, unplace_b)
     fetch(unpack_in, unpack)
     for copy in loads[:early]:
         copy.wait()
     out_halo[0] = dot(pack[...], both[0]).astype(BF)
     meet()
-    coming = [halo(p, -1, out_halo, in_halo, hsend, hrecv) for p in range(2)]
-    for copy in coming[0]:
-        copy.start()
+    coming = [halo(w, -1, out_halo, in_halo, hsend, hrecv) for w in range(4)]
+
+    def send_in(w):
+        for copy in coming[w]:
+            copy.start()
+
+    send_in(0)
+    send_in(1)
     out_halo[1] = dot(pack[...], both[1]).astype(BF)
-    for copy in coming[1]:
-        copy.start()
+    send_in(3)
+    send_in(2)
     for copy in loads[early:]:
         copy.wait()
     for g in range(2):
@@ -373,16 +383,19 @@
     mask = head_mask(BF)
     maskf = head_mask(F32)
 
-    def arrive(p):
-        in_halo[p, 0:224] = out_halo[p, 0:224]
-        for copy in coming[p]:
+    def arrive(w):
+        p, loc = w // 2, w % 2
+        at, count = KEPT[loc]
+        in_halo[p, at : at + count] = out_halo[p, at : at + count]
+        for copy in coming[w]:
             copy.wait_recv()
-        tok[pair_rows(p), :] = dot(place_m[0:288, :], in_halo[p]).astype(BF)
-        cot[pair_rows(p), :] = dot(place_m[288:576, :], in_halo[p]).astype(BF)
-        project(p, tok, cot, w_qkv, w_proj_t, hat, normed, inv, q, k, v, dc)
-
-    def attention(p, g):
-        attend(p, g, lat_last, lon_last, mask, maskf, q, k, v, dc, qs, cs, pt, st, sf, df, ctx, dqkv)
+        placed = dot((place_a, place_b)[loc][...], in_halo[p, SPAN[loc]]).astype(BF)
+        tok[144 * w : 144 * w + 144, :] = placed[0:144]
+        cot[144 * w : 144 * w + 144, :] = placed[144:288]
+        project(w, tok, cot, w_qkv, w_proj_t, hat, normed, inv, q, k, v, dc)
+
+    def attention(w, groups):
+        attend(w, groups, lat_last, lon_last, mask, maskf, q, k, v, dc, qs, cs, pt, st, sf, df, ctx, dqkv)
 
     def swap_in(g):
         return core_swap(grad.at[g, 1 - core], swapped.at[g], swap_send.at[g], swap_recv.at[g])
@@ -420,7 +433,6 @@
         for b in range(2):
             drain(parts2.at[b, pl.ds(0, 15)], recv.at[3, b])
             gather_first(b, total.at[core], wide_send, wide_recv)
-        send_back(1)
         for b in range(2):
             core_out(b, 0).start()
         for i in (1, 3, 2):
@@ -444,9 +456,11 @@
                 drain(total.at[core, b, pl.ds(0, 16)], wide_send.at[b, i])
 
     def back(p):
-        in_back[p, 0:224] = out_back[p, 0:224]
-        for copy in going[p]:
-            copy.wait_recv()
+        for w in (2 * p, 2 * p + 1):
+            at, count = KEPT[w % 2]
+            in_back[p, at : at + count] = out_back[p, at : at + count]
+            for copy in going[w]:
+                copy.wait_recv()
         for half in range(2):
             for level in range(2):
                 at = 144 * ((2 * p + 1 + level) % 4)
@@ -454,46 +468,47 @@
                 d = dot(unpack[rows, :], in_back[p]).astype(BF)
                 moved[half, at : at + 144, :] = (both[p, rows, :].astype(F32) + d.astype(F32)).astype(BF)
 
-    going = [halo(p, 1, out_back, in_back, bsend, brecv) for p in range(2)]
+    going = [halo(w, 1, out_back, in_back, bsend, brecv) for w in range(4)]
 
     def leave(p):
         finish(p, w_qkv_t, w_proj, hat, inv, ctx, dqkv, done)
-        out_back[p] = dot(unplace[...], done[p]).astype(BF)
 
     def send_back(p):
-        for copy in going[p]:
-            copy.start()
-
-    arrive(0)
-
-    @pl.loop(0, 2)
-    def _(g):
-        attention(0, g)
-
+        for w in (2 * p, 2 * p + 1):
+            unplace = (unplace_a, unplace_b)[w % 2]
+            out_back[p, SPAN[w % 2]] = dot(unplace[...], done[w]).astype(BF)
+            for copy in going[w]:
+                copy.start()
+
+    for w in (0, 1):
+        arrive(w)
+        attention(w, (0, 1))
     leave(0)
     send_back(0)
-    arrive(1)
-    attention(1, 0)
+    arrive(3)
+    attention(3, (0, 1))
+    arrive(2)
+    attention(2, (0,))
     weight_gradients(0, normed, cot, ctx, dqkv, grad)
     swap_in(0).start()
-    attention(1, 1)
+    attention(2, (1,))
     sum_first(0)
     weight_gradients(1, normed, cot, ctx, dqkv, grad)
     swap_in(1).start()
-    finish(1, w_qkv_t, w_proj, hat, inv, ctx, dqkv, done)
+    leave(1)
     sum_first(1)
-    out_back[1] = dot(unplace[...], done[1]).astype(BF)
     back(0)
     sum_second()
     spread_second()
+    send_back(1)
     spread_first()
     store_half(core, 0).start()
     back(1)
     for copy in store_moved():
         copy.start()
     drain_sends()
-    for p in range(2):
-        for copy in coming[p] + going[p]:
+    for w in range(4):
+        for copy in coming[w] + going[w]:
             copy.wait_send()
     for b in range(2):
         for i in range(4):
@@ -513,7 +528,7 @@
             jax.ShapeDtypeStruct((576, 512), BF),
             jax.ShapeDtypeStruct((2, 2, 64, 2, 16, 128), BF),
         ),
-        in_specs=[hbm] * 8,
+        in_specs=[hbm] * 10,
         out_specs=(hbm,) * 3,
         scratch_shapes=[
             pltpu.VMEM((2, 576, 512), BF),
@@ -523,8 +538,10 @@
             pltpu.VMEM((1536, 512), BF),
             pltpu.VMEM((512, 512), BF),
             pltpu.VMEM((ROWS, 576), BF),
-            pltpu.VMEM((576, ROWS), BF),
-            pltpu.VMEM((ROWS, 576), BF),
+            pltpu.VMEM((288, 288), BF),
+            pltpu.VMEM((288, 320), BF),
+            pltpu.VMEM((288, 288), BF),
+            pltpu.VMEM((320, 288), BF),
             pltpu.VMEM((576, ROWS), BF),
             pltpu.VMEM((2, ROWS, 512), BF),
             pltpu.VMEM((2, ROWS, 512), BF),
@@ -547,7 +564,7 @@
             pltpu.VMEM((2, 144, 1152), F32),
             pltpu.VMEM((576, 512), BF),
             pltpu.VMEM((576, 1536), BF),
-            pltpu.VMEM((2, 576, 512), BF),
+            pltpu.VMEM((4, 288, 512), BF),
             pltpu.VMEM((2, 2, 2, 64, 16, 128), BF),
             pltpu.VMEM((2, 2, 64, 16, 128), BF),
             pltpu.VMEM((2, 2, 64, 16, 128), BF),
@@ -565,10 +582,10 @@
             dma((2, 4)),
             dma((2, 4)),
             dma((2, 4)),
-            dma((2, 3)),
-            dma((2, 3)),
-            dma((2, 3)),
-            dma((2, 3)),
+            dma((4, 3)),
+            dma((4, 3)),
+            dma((4, 3)),
+            dma((4, 3)),
         ],
         compiler_params=pltpu.CompilerParams(
             vmem_limit_bytes=56 * 2**20, collective_id=0, has_side_effects=True
@@ -579,11 +596,13 @@
 
 def hand_over(moved_a, moved_b, total_in, out_a, out_b, gqkv_out, gproj_out, moved, total, gqkv, gproj, load, store):
     loads = [
-        pltpu.make_async_copy(total_in.at[0], total.at[0], load.at[0]),
-        pltpu.make_async_copy(total_in.at[1], total.at[1], load.at[1]),
-        pltpu.make_async_copy(moved_a, moved.at[0], load.at[2]),
-        pltpu.make_async_copy(moved_b, moved.at[1], load.at[3]),
+        pltpu.make_async_copy(moved_a, moved.at[0], load.at[0]),
+        pltpu.make_async_copy(moved_b, moved.at[1], load.at[1]),
     ]
+    for half in range(2):
+        for b in range(2):
+            src, dst = total_in.at[half, b], total.at[half, b]
+            loads.append(pltpu.make_async_copy(src, dst, load.at[2 + 2 * half + b]))
     for copy in loads:
         copy.start()
     stores = []
@@ -593,9 +612,7 @@
         copy.start()
         stores.append(copy)
 
-    for part in range(3):
-        if part != 1:
-            loads[part // 2].wait()
+    def widen(part):
         for g in range(2):
             for b in range(2):
                 at = 512 * part + 256 * g + 128 * b
@@ -603,6 +620,18 @@
                 gqkv[:, at : at + 128] = total[part // 2, b, rows, g].reshape(512, 128).astype(F32)
         at = pl.ds(512 * part, 512)
         write(gqkv.at[:, at], gqkv_out.at[:, at])
+
+    loads[0].wait()
+    write(moved.at[0], out_a)
+    loads[1].wait()
+    write(moved.at[1], out_b)
+    for copy in loads[2:4]:
+        copy.wait()
+    widen(0)
+    widen(1)
+    for copy in loads[4:6]:
+        copy.wait()
+    widen(2)
     for g in range(2):
         for b in range(2):
             for side in range(2):
@@ -610,10 +639,6 @@
                 piece = total[1, b, 32 + 16 * side : 48 + 16 * side, g].reshape(256, 128)
                 gproj[256 * g : 256 * g + 256, at : at + 128] = piece.astype(F32)
     write(gproj, gproj_out)
-    loads[2].wait()
-    write(moved.at[0], out_a)
-    loads[3].wait()
-    write(moved.at[1], out_b)
     for copy in stores:
         copy.wait()
 
@@ -637,7 +662,7 @@
             pltpu.VMEM((2, 2, 64, 2, 16, 128), BF),
             pltpu.VMEM((512, 1536), F32),
             pltpu.VMEM((512, 512), F32),
-            pltpu.SemaphoreType.DMA((4,)),
+            pltpu.SemaphoreType.DMA((6,)),
             pltpu.SemaphoreType.DMA((6,)),
         ],
         compiler_params=pltpu.CompilerParams(vmem_limit_bytes=56 * 2**20),

time: 74.3 us -> 72.3 us (0.973)
  Pallas kernels: 73.3 us -> 71.4 us
    pallas_call x1, Pallas kernels: 69.5 us -> 67.6 us  [block(): pl.pallas_call(kernel, out_shape=(jax.ShapeDtypeStruct((576, 512), BF), j...]
where the time goes in v7:
time: 72.3 us; the launch traced here: 72.2 us
  Pallas kernels  71.4 us (99%)
  between operations  0.8 us (1%)
    pallas_call x1, Pallas kernels, block(): pl.pallas_call(kernel, out_shape=(jax.ShapeDtypeStruct((576, 512), BF), j...  67.6 us
    pallas_call x1, Pallas kernels, body(): pl.pallas_call(hand_over, out_shape=(jax.ShapeDtypeStruct((576, 512), BF)...  3.8 us

profile of v7, /device:TPU:1, one launch (start us, length us, event | category | flops | bytes accessed | tf_op | source)
XLA Modules:
  0.0 72.2 jit_solution(6332863580269081471)
XLA Ops:
  0.6 67.6 %window_block.1 = (bf16[576,512]{1,0:T(8,128)(2,1)}, bf16[576,512]{1,0:T(8,128)(2,1)}, bf16[2,2,64,2,16,128]{5,4,3,2,1,0:T(8,128)(2,1)}) custom-call(bf16[576,512]{1,0:T(8,128)(2,1)} %bitcast.4, bf16[576,512]{1,0:T(8,128)(2,1)} %bitcast.5, bf16[512,1536]{1,0:T(8,128)(2,1)} %w_qkv_in.1, bf16[512,512]{1,0:T(8,128)(2,1)} %w_proj_in.1, ...), custom_call_target="tpu_custom_call" | custom-call | tf_op jit(solution)/shard_map/window_block/pallas_call | solution.py:524
  68.2 3.8 %hand_over.1 = (bf16[576,512]{1,0:T(8,128)(2,1)}, bf16[576,512]{1,0:T(8,128)(2,1)}, f32[512,1536]{1,0:T(8,128)}, f32[512,512]{1,0:T(8,128)}) custom-call(bf16[576,512]{1,0:T(8,128)(2,1)} %get-tuple-element.11.moved_a, bf16[576,512]{1,0:T(8,128)(2,1)} %get-tuple-element.12.moved_b, bf16[2,2,64,2,16,128]{5,4,3,2,1,0:T(8,128)(2,1)} %get-tuple-element.13.total_in), custom_call_target="tpu_custom_call" | custom-call | tf_op jit(solution)/shard_map/hand_over/pallas_call | solution.py:650

commit v8 on v7

--- a/solution.py
+++ b/solution.py
@@ -283,7 +283,7 @@
             ).start()
 
 
-def scatter_second(mixed, parts, send, recv):
+def scatter_second(g, mixed, parts, send, recv):
     for b in range(2):
         at = second_at(b)
 
@@ -291,16 +291,16 @@
         def _(t):
             to = at ^ (15 - t)
             pltpu.make_async_remote_copy(
-                src_ref=mixed.at[b, to], dst_ref=parts.at[b, at],
+                src_ref=mixed.at[b, to, g], dst_ref=parts.at[b, at, g],
                 send_sem=send.at[b], recv_sem=recv.at[b],
                 device_id=second_device(b, to), device_id_type=MESH,
             ).start()
 
 
-def gather_second(total, send, recv):
+def gather_second(g, total, send, recv):
     for b in range(2):
         at = second_at(b)
-        piece = total.at[b, first_at(b) * 16 + at]
+        piece = total.at[b, first_at(b) * 16 + at, g]
 
         @pl.loop(0, 15)
         def _(t):
@@ -310,12 +310,12 @@
             ).start()
 
 
-def gather_first(b, total, send, recv):
+def gather_first(g, b, total, send, recv):
     at = first_at(b)
-    piece = total.at[b, pl.ds(at * 16, 16)]
+    piece = total.at[b, pl.ds(at * 16, 16), g]
     for k in (2, 1, 3):
         pltpu.make_async_remote_copy(
-            src_ref=piece, dst_ref=piece, send_sem=send.at[b, k], recv_sem=recv.at[b, k],
+            src_ref=piece, dst_ref=piece, send_sem=send.at[g, b, k], recv_sem=recv.at[g, b, k],
             device_id=first_device(b, at ^ k), device_id_type=MESH,
         ).start()
 
@@ -328,7 +328,6 @@
     grad, swapped, mixed, parts, mixed2, parts2, total, load, store, swap_send, swap_recv, send, recv, core_send, core_recv, wide_send, wide_recv, hsend, hrecv, bsend, brecv,
 ):
     x, y, z, core = place()
-    greet()
     loads = []
 
     def fetch(src, dst):
@@ -336,15 +335,20 @@
         copy.start()
         loads.append(copy)
 
-    for p in range(2):
+    def fetch_tiles(p):
         for half, src in enumerate((tokens, cotangent)):
             for level in range(2):
                 fetch(
                     src.at[pl.ds(144 * ((2 * p + 1 + level) % 4), 144)],
                     both.at[p, pl.ds(288 * half + 144 * level, 144)],
                 )
+
     fetch(pack_in, pack)
+    fetch_tiles(0)
     early = len(loads)
+    greet()
+    fetch_tiles(1)
+    middle = len(loads)
     fetch(place_0, place_a)
     fetch(place_1, place_b)
     fetch(w_qkv_in, w_qkv)
@@ -354,7 +358,7 @@
     fetch(unpack_in, unpack)
     for copy in loads[:early]:
         copy.wait()
-    out_halo[0] = dot(pack[...], both[0]).astype(BF)
+    out_halo[0, SPAN[0]] = dot(pack[SPAN[0], :], both[0]).astype(BF)
     meet()
     coming = [halo(w, -1, out_halo, in_halo, hsend, hrecv) for w in range(4)]
 
@@ -363,11 +367,14 @@
             copy.start()
 
     send_in(0)
+    out_halo[0, SPAN[1]] = dot(pack[SPAN[1], :], both[0]).astype(BF)
     send_in(1)
+    for copy in loads[early:middle]:
+        copy.wait()
     out_halo[1] = dot(pack[...], both[1]).astype(BF)
     send_in(3)
     send_in(2)
-    for copy in loads[early:]:
+    for copy in loads[middle:]:
         copy.wait()
     for g in range(2):
         for part in range(3):
@@ -408,37 +415,37 @@
             at = first_at(b)
             parts[g, b, at] = mixed[g, b, pl.ds(at * 16, 16)]
 
-    def sum_second():
-        for b in range(2):
-            for g in range(2):
-                drain(parts.at[g, b, pl.ds(0, 3)], recv.at[g, b])
-                mixed2[b, :, g] = jnp.sum(parts[g, b].astype(F32), axis=0).astype(BF)
-        scatter_second(mixed2, parts2, send.at[2], recv.at[2])
+    def sum_second(g):
+        for b in range(2):
+            drain(parts.at[g, b, pl.ds(0, 3)], recv.at[g, b])
+            mixed2[b, :, g] = jnp.sum(parts[g, b].astype(F32), axis=0).astype(BF)
+        scatter_second(g, mixed2, parts2, send.at[2 + g], recv.at[2 + g])
         for b in range(2):
             at = second_at(b)
-            parts2[b, at] = mixed2[b, at]
-
-    def spread_second():
-        for b in range(2):
-            drain(parts2.at[b, pl.ds(0, 15)], recv.at[2, b])
-            final = jnp.sum(parts2[b].astype(F32), axis=0) * NORM
-            total[core, b, first_at(b) * 16 + second_at(b)] = final.astype(BF)
-        gather_second(total.at[core], send.at[3], recv.at[3])
-
-    def core_out(b, i):
-        part = total.at[core, b, pl.ds((first_at(b) ^ i) * 16, 16)]
-        return core_swap(part, part, core_send.at[b, i], core_recv.at[b, i])
-
-    def spread_first():
-        for b in range(2):
-            drain(parts2.at[b, pl.ds(0, 15)], recv.at[3, b])
-            gather_first(b, total.at[core], wide_send, wide_recv)
-        for b in range(2):
-            core_out(b, 0).start()
+            parts2[b, at, g] = mixed2[b, at, g]
+
+    def spread_second(g):
+        for b in range(2):
+            drain(parts2.at[b, pl.ds(0, 15), g], recv.at[2 + g, b])
+            final = jnp.sum(parts2[b, :, g].astype(F32), axis=0) * NORM
+            total[core, b, first_at(b) * 16 + second_at(b), g] = final.astype(BF)
+        gather_second(g, total.at[core], send.at[4 + g], recv.at[4 + g])
+
+    def core_out(g, b, i):
+        part = total.at[core, b, pl.ds((first_at(b) ^ i) * 16, 16), g]
+        return core_swap(part, part, core_send.at[g, b, i], core_recv.at[g, b, i])
+
+    def spread_first(g):
+        for b in range(2):
+            drain(parts2.at[b, pl.ds(0, 15), g], recv.at[4 + g, b])
+            gather_first(g, b, total.at[core], wide_send, wide_recv)
+            core_out(g, b, 0).start()
+
+    def spread_core(g):
         for i in (1, 3, 2):
             for b in range(2):
-                drain(total.at[core, b, pl.ds(0, 16)], wide_recv.at[b, i])
-                core_out(b, i).start()
+                drain(total.at[core, b, pl.ds(0, 16), g], wide_recv.at[g, b, i])
+                core_out(g, b, i).start()
 
     def store_half(half, i):
         return pltpu.make_async_copy(total.at[half], total_out.at[half], store.at[2 + i])
@@ -448,12 +455,13 @@
         return [pltpu.make_async_copy(moved.at[i], outs[i], store.at[i]) for i in range(2)]
 
     def drain_sends():
-        for b in range(2):
-            for g in range(2):
+        for g in range(2):
+            for b in range(2):
                 drain(parts.at[g, b, pl.ds(0, 3)], send.at[g, b])
-                drain(parts2.at[b, pl.ds(0, 15)], send.at[2 + g, b])
-            for i in range(1, 4):
-                drain(total.at[core, b, pl.ds(0, 16)], wide_send.at[b, i])
+                drain(parts2.at[b, pl.ds(0, 15), g], send.at[2 + g, b])
+                drain(parts2.at[b, pl.ds(0, 15), g], send.at[4 + g, b])
+                for i in range(1, 4):
+                    drain(total.at[core, b, pl.ds(0, 16), g], wide_send.at[g, b, i])
 
     def back(p):
         for w in (2 * p, 2 * p + 1):
@@ -498,10 +506,15 @@
     leave(1)
     sum_first(1)
     back(0)
-    sum_second()
-    spread_second()
+    sum_second(0)
+    sum_second(1)
+    spread_second(0)
+    spread_second(1)
+    spread_first(0)
+    spread_first(1)
     send_back(1)
-    spread_first()
+    spread_core(0)
+    spread_core(1)
     store_half(core, 0).start()
     back(1)
     for copy in store_moved():
@@ -510,9 +523,10 @@
     for w in range(4):
         for copy in coming[w] + going[w]:
             copy.wait_send()
-    for b in range(2):
-        for i in range(4):
-            core_out(b, i).wait()
+    for g in range(2):
+        for b in range(2):
+            for i in range(4):
+                core_out(g, b, i).wait()
     store_half(1 - core, 1).start()
     for copy in store_moved() + [store_half(core, 0), store_half(1 - core, 1)]:
         copy.wait()
@@ -576,12 +590,12 @@
             dma((4,)),
             dma((2,)),
             dma((2,)),
-            dma((4, 2)),
-            dma((4, 2)),
-            dma((2, 4)),
-            dma((2, 4)),
-            dma((2, 4)),
-            dma((2, 4)),
+            dma((6, 2)),
+            dma((6, 2)),
+            dma((2, 2, 4)),
+            dma((2, 2, 4)),
+            dma((2, 2, 4)),
+            dma((2, 2, 4)),
             dma((4, 3)),
             dma((4, 3)),
             dma((4, 3)),

time: 72.3 us -> 72.1 us (level)
  no operation moved by 1% of the time
where the time goes in v8:
time: 72.1 us; the launch traced here: 71.9 us
  Pallas kernels  71.1 us (99%)
  between operations  0.8 us (1%)
    pallas_call x1, Pallas kernels, block(): pl.pallas_call(kernel, out_shape=(jax.ShapeDtypeStruct((576, 512), BF), j...  67.3 us
    pallas_call x1, Pallas kernels, body(): pl.pallas_call(hand_over, out_shape=(jax.ShapeDtypeStruct((576, 512), BF)...  3.8 us

profile of v8, /device:TPU:1, one launch (start us, length us, event | category | flops | bytes accessed | tf_op | source)
XLA Modules:
  0.0 71.9 jit_solution(7980223777571572696)
XLA Ops:
  0.6 67.3 %window_block.1 = (bf16[576,512]{1,0:T(8,128)(2,1)}, bf16[576,512]{1,0:T(8,128)(2,1)}, bf16[2,2,64,2,16,128]{5,4,3,2,1,0:T(8,128)(2,1)}) custom-call(bf16[576,512]{1,0:T(8,128)(2,1)} %bitcast.4, bf16[576,512]{1,0:T(8,128)(2,1)} %bitcast.5, bf16[512,1536]{1,0:T(8,128)(2,1)} %w_qkv_in.1, bf16[512,512]{1,0:T(8,128)(2,1)} %w_proj_in.1, ...), custom_call_target="tpu_custom_call" | custom-call | tf_op jit(solution)/shard_map/window_block/pallas_call | solution.py:538
  68.0 3.8 %hand_over.1 = (bf16[576,512]{1,0:T(8,128)(2,1)}, bf16[576,512]{1,0:T(8,128)(2,1)}, f32[512,1536]{1,0:T(8,128)}, f32[512,512]{1,0:T(8,128)}) custom-call(bf16[576,512]{1,0:T(8,128)(2,1)} %get-tuple-element.11.moved_a, bf16[576,512]{1,0:T(8,128)(2,1)} %get-tuple-element.12.moved_b, bf16[2,2,64,2,16,128]{5,4,3,2,1,0:T(8,128)(2,1)} %get-tuple-element.13.total_in), custom_call_target="tpu_custom_call" | custom-call | tf_op jit(solution)/shard_map/hand_over/pallas_call | solution.py:664

commit v9 on v8

--- a/solution.py
+++ b/solution.py
@@ -481,18 +481,18 @@
     def leave(p):
         finish(p, w_qkv_t, w_proj, hat, inv, ctx, dqkv, done)
 
-    def send_back(p):
-        for w in (2 * p, 2 * p + 1):
-            unplace = (unplace_a, unplace_b)[w % 2]
-            out_back[p, SPAN[w % 2]] = dot(unplace[...], done[w]).astype(BF)
-            for copy in going[w]:
-                copy.start()
+    def send_back(w):
+        unplace = (unplace_a, unplace_b)[w % 2]
+        out_back[w // 2, SPAN[w % 2]] = dot(unplace[...], done[w]).astype(BF)
+        for copy in going[w]:
+            copy.start()
 
     for w in (0, 1):
         arrive(w)
         attention(w, (0, 1))
     leave(0)
     send_back(0)
+    send_back(1)
     arrive(3)
     attention(3, (0, 1))
     arrive(2)
@@ -504,15 +504,16 @@
     weight_gradients(1, normed, cot, ctx, dqkv, grad)
     swap_in(1).start()
     leave(1)
+    send_back(3)
     sum_first(1)
     back(0)
     sum_second(0)
     sum_second(1)
     spread_second(0)
     spread_second(1)
+    send_back(2)
     spread_first(0)
     spread_first(1)
-    send_back(1)
     spread_core(0)
     spread_core(1)
     store_half(core, 0).start()

time: 72.1 us -> 69.5 us (0.964)
  Pallas kernels: 71.1 us -> 68.6 us
    pallas_call x1, Pallas kernels: 67.3 us -> 64.8 us  [block(): pl.pallas_call(kernel, out_shape=(jax.ShapeDtypeStruct((576, 512), BF), j...]
where the time goes in v9:
time: 69.5 us; the launch traced here: 69.4 us
  Pallas kernels  68.6 us (99%)
  between operations  0.8 us (1%)
    pallas_call x1, Pallas kernels, block(): pl.pallas_call(kernel, out_shape=(jax.ShapeDtypeStruct((576, 512), BF), j...  64.8 us
    pallas_call x1, Pallas kernels, body(): pl.pallas_call(hand_over, out_shape=(jax.ShapeDtypeStruct((576, 512), BF)...  3.8 us

profile of v9, /device:TPU:1, one launch (start us, length us, event | category | flops | bytes accessed | tf_op | source)
XLA Modules:
  0.0 69.4 jit_solution(847794834656770951)
XLA Ops:
  0.6 64.8 %window_block.1 = (bf16[576,512]{1,0:T(8,128)(2,1)}, bf16[576,512]{1,0:T(8,128)(2,1)}, bf16[2,2,64,2,16,128]{5,4,3,2,1,0:T(8,128)(2,1)}) custom-call(bf16[576,512]{1,0:T(8,128)(2,1)} %bitcast.4, bf16[576,512]{1,0:T(8,128)(2,1)} %bitcast.5, bf16[512,1536]{1,0:T(8,128)(2,1)} %w_qkv_in.1, bf16[512,512]{1,0:T(8,128)(2,1)} %w_proj_in.1, ...), custom_call_target="tpu_custom_call" | custom-call | tf_op jit(solution)/shard_map/window_block/pallas_call | solution.py:539
  65.4 3.8 %hand_over.1 = (bf16[576,512]{1,0:T(8,128)(2,1)}, bf16[576,512]{1,0:T(8,128)(2,1)}, f32[512,1536]{1,0:T(8,128)}, f32[512,512]{1,0:T(8,128)}) custom-call(bf16[576,512]{1,0:T(8,128)(2,1)} %get-tuple-element.11.moved_a, bf16[576,512]{1,0:T(8,128)(2,1)} %get-tuple-element.12.moved_b, bf16[2,2,64,2,16,128]{5,4,3,2,1,0:T(8,128)(2,1)} %get-tuple-element.13.total_in), custom_call_target="tpu_custom_call" | custom-call | tf_op jit(solution)/shard_map/hand_over/pallas_call | solution.py:665

commit v10 on v9

--- a/solution.py
+++ b/solution.py
@@ -144,18 +144,16 @@
         results(g)
 
 
-def finish(p, w_qkv_t, w_proj, hat, inv, ctx, dqkv, done):
-    rows = pair_rows(p)
+def finish(w, w_qkv_t, w_proj, hat, inv, ctx, dqkv, done):
+    rows = slice(144 * w, 144 * w + 144)
     a = dot(ctx[rows, :], w_proj[...]).astype(BF)
     d = dot(dqkv[rows, :], w_qkv_t[...])
     h = hat[rows, :]
     d = d - jnp.mean(d, axis=1, keepdims=True) - h * jnp.mean(d * h, axis=1, keepdims=True)
     scale = jnp.concatenate([inv[rows, :]] * 4, axis=1)
     d = (d * scale).astype(BF)
-    for i in range(2):
-        own = slice(144 * i, 144 * i + 144)
-        done[2 * p + i, 0:144, :] = a[own]
-        done[2 * p + i, 144:288, :] = d[own]
+    done[w, 0:144, :] = a
+    done[w, 144:288, :] = d
 
 
 def labels(w, lat_last, lon_last):
@@ -478,8 +476,8 @@
 
     going = [halo(w, 1, out_back, in_back, bsend, brecv) for w in range(4)]
 
-    def leave(p):
-        finish(p, w_qkv_t, w_proj, hat, inv, ctx, dqkv, done)
+    def leave(w):
+        finish(w, w_qkv_t, w_proj, hat, inv, ctx, dqkv, done)
 
     def send_back(w):
         unplace = (unplace_a, unplace_b)[w % 2]
@@ -492,9 +490,12 @@
         attention(w, (0, 1))
     leave(0)
     send_back(0)
+    leave(1)
     send_back(1)
     arrive(3)
     attention(3, (0, 1))
+    leave(3)
+    send_back(3)
     arrive(2)
     attention(2, (0,))
     weight_gradients(0, normed, cot, ctx, dqkv, grad)
@@ -503,15 +504,14 @@
     sum_first(0)
     weight_gradients(1, normed, cot, ctx, dqkv, grad)
     swap_in(1).start()
-    leave(1)
-    send_back(3)
     sum_first(1)
+    leave(2)
     back(0)
     sum_second(0)
     sum_second(1)
+    send_back(2)
     spread_second(0)
     spread_second(1)
-    send_back(2)
     spread_first(0)
     spread_first(1)
     spread_core(0)

time: 69.5 us -> 68.1 us (0.980)
  Pallas kernels: 68.6 us -> 67.2 us
    pallas_call x1, Pallas kernels: 64.8 us -> 63.4 us  [block(): pl.pallas_call(kernel, out_shape=(jax.ShapeDtypeStruct((576, 512), BF), j...]
where the time goes in v10:
time: 68.1 us; the launch traced here: 68 us
  Pallas kernels  67.2 us (99%)
  between operations  0.8 us (1%)
    pallas_call x1, Pallas kernels, block(): pl.pallas_call(kernel, out_shape=(jax.ShapeDtypeStruct((576, 512), BF), j...  63.4 us
    pallas_call x1, Pallas kernels, body(): pl.pallas_call(hand_over, out_shape=(jax.ShapeDtypeStruct((576, 512), BF)...  3.8 us

profile of v10, /device:TPU:1, one launch (start us, length us, event | category | flops | bytes accessed | tf_op | source)
XLA Modules:
  0.0 68.0 jit_solution(9770720416984445797)
XLA Ops:
  0.6 63.4 %window_block.1 = (bf16[576,512]{1,0:T(8,128)(2,1)}, bf16[576,512]{1,0:T(8,128)(2,1)}, bf16[2,2,64,2,16,128]{5,4,3,2,1,0:T(8,128)(2,1)}) custom-call(bf16[576,512]{1,0:T(8,128)(2,1)} %bitcast.4, bf16[576,512]{1,0:T(8,128)(2,1)} %bitcast.5, bf16[512,1536]{1,0:T(8,128)(2,1)} %w_qkv_in.1, bf16[512,512]{1,0:T(8,128)(2,1)} %w_proj_in.1, ...), custom_call_target="tpu_custom_call" | custom-call | tf_op jit(solution)/shard_map/window_block/pallas_call | solution.py:539
  64.0 3.8 %hand_over.1 = (bf16[576,512]{1,0:T(8,128)(2,1)}, bf16[576,512]{1,0:T(8,128)(2,1)}, f32[512,1536]{1,0:T(8,128)}, f32[512,512]{1,0:T(8,128)}) custom-call(bf16[576,512]{1,0:T(8,128)(2,1)} %get-tuple-element.11.moved_a, bf16[576,512]{1,0:T(8,128)(2,1)} %get-tuple-element.12.moved_b, bf16[2,2,64,2,16,128]{5,4,3,2,1,0:T(8,128)(2,1)} %get-tuple-element.13.total_in), custom_call_target="tpu_custom_call" | custom-call | tf_op jit(solution)/shard_map/hand_over/pallas_call | solution.py:665
